TPU v7x, 128 devices: a whole 4x4x4 slice. The times are simulated.
128 devices in a mesh: row: 8 (over z, core), height: 16 (over y, x).
Axes of the slice: x: 4, y: 4, z: 4, core: 2. Of those that a mesh axis runs over, the one named last changes fastest.
Arguments:
- heat_source_points: float32 [8, 8, 8, 8, 16, 128], P(None, None, None, 'row', 'height'), may hold values from -6 to 6
- conductivity: float32 [8, 16, 128], P('row', 'height'), may hold values from 0.5 to 8
- solid_element_marks: int32 [8, 16, 128], P('row', 'height'), may hold values 0 or 1
- face_owner: int32 [65536, 1], P(('row', 'height')), may hold values from 0 to 127; in each aligned block of 512 rows (0 to 511, 512 to 1023, ...) at most 16 rows name the same one
- face_element: int32 [65536], P(('row', 'height')), may hold values from 0 to 127
- face_side: int32 [65536], P(('row', 'height')), may hold values from 0 to 5
- owner_element: int32 [65536], P(('row', 'height')), may hold values from 0 to 127
Outputs:
- temperature: float32 [8, 8, 8, 8, 16, 128], P(None, None, None, 'row', 'height')
- residual: float32 [8, 8, 8, 8, 16, 128], P(None, None, None, 'row', 'height')
- interface_load: float32 [128, 8, 16, 128], P(None, 'row', 'height')
Inputs may be any that keep to these rules, and one draw needn't show every extreme that they name: `face_owner`: among the 512 faces listed on one device, at most 16 name the same owner device, and some device reaches 16.
All inputs are finite; a program needn't handle non-finite values. No bound on the sum of `solid_element_marks` on one device may be relied on, other than what follows from the above.
Results may differ from a plain program's by a relative error of at most 0.0017.
Values sent between devices are 32-bit elements; how exact they have to be, the bound alone decides.
No kernel may reach another device: no remote copies, remote signals or barrier semaphores. Data moves between devices by JAX's collectives and lax.ppermute only.
A program may use at most 128 MiB of HBM per device.

v0:
```python
import functools

import jax
import jax.numpy as jnp
import numpy as np
from jax import lax
from jax.experimental import pallas as pl
from jax.experimental.pallas import tpu as pltpu
from jax.sharding import PartitionSpec as P

ITERS = 8
HEAT_AIR = 0.02
HEAT_SOLID = 0.08
GLL_INNER = (
    -0.8717401485096066,
    -0.5917001814331423,
    -0.2092992179024789,
    0.2092992179024789,
    0.5917001814331423,
    0.8717401485096066,
)
F32 = jnp.float32
NX, NZ, NY = 8, 16, 128
FIELD = (8, 8, 8, NY)
FACE = (8, 8, NY)
COARSE = (NZ, NX, NY)


def legendre_values(points_in, degree):
    before = points_in * 0.0 + 1.0
    current = points_in * 1.0
    for order_now in range(1, degree):
        following = ((2 * order_now + 1) * points_in * current - order_now * before) / (
            order_now + 1
        )
        before = current
        current = following
    return current


def gll_tables():
    poly_order = 7
    gll_nodes = np.array((-1.0,) + GLL_INNER + (1.0,))
    edge_values = legendre_values(gll_nodes, poly_order)
    gll_weights = 2.0 / (poly_order * (poly_order + 1) * edge_values**2)
    diff_table = np.zeros((8, 8))
    for row_index in range(8):
        for col_index in range(8):
            if row_index != col_index:
                diff_table[row_index, col_index] = edge_values[row_index] / (
                    edge_values[col_index] * (gll_nodes[row_index] - gll_nodes[col_index])
                )
    diff_table[0, 0] = -poly_order * (poly_order + 1) / 4.0
    diff_table[7, 7] = poly_order * (poly_order + 1) / 4.0
    return (gll_weights, diff_table)


W_, D_ = gll_tables()
K_ = D_.T @ np.diag(W_) @ D_
S_ = np.sum(D_**2 * W_[:, None], axis=0)
W = [float(v) for v in W_]
SD = [float(v) for v in S_]
E = 7


def kvec(vals):
    k = lax.broadcasted_iota(jnp.int32, (8, NY), 0)
    out = jnp.full((8, NY), float(vals[0]), F32)
    for n in range(1, 8):
        out = jnp.where(k == n, jnp.float32(float(vals[n])), out)
    return out


def apply1d(v, mat):
    ev = [v[a] + v[7 - a] for a in range(4)]
    od = [v[a] - v[7 - a] for a in range(4)]
    out = [None] * 8
    for i in range(4):
        s = d = None
        for a in range(4):
            cs = float(0.5 * (mat[i, a] + mat[i, 7 - a]))
            cd = float(0.5 * (mat[i, a] - mat[i, 7 - a]))
            s = cs * ev[a] if s is None else s + cs * ev[a]
            d = cd * od[a] if d is None else d + cd * od[a]
        out[i] = s + d
        out[7 - i] = s - d
    return out


def place(pos_ref):
    ix, iz = pos_ref[0], pos_ref[1]
    has = (ix > 0, ix < NX - 1, iz > 0, iz < NZ - 1)
    frac = tuple(jnp.where(h, jnp.float32(0.5), jnp.float32(1.0)) for h in has)
    even = (lax.rem(ix, 2) == 0, lax.rem(iz, 2) == 0)
    return ix, iz, has, frac, even


def own_mult():
    k = lax.broadcasted_iota(jnp.int32, (8, NY), 0)
    y = lax.broadcasted_iota(jnp.int32, (8, NY), 1)
    shared = ((k == 0) & (y > 0)) | ((k == E) & (y < NY - 1))
    return jnp.where(shared, jnp.float32(0.5), jnp.float32(1.0))


def field_sum(get, frac):
    total = None
    for i in range(8):
        mid = get(i, 1)
        for j in range(2, 7):
            mid = mid + get(i, j)
        row = mid + frac[2] * get(i, 0) + frac[3] * get(i, E)
        if i == 0:
            row = frac[0] * row
        elif i == E:
            row = frac[1] * row
        total = row if total is None else total + row
    return total


def assemble_aisle(ref):
    low, high = ref[:, :, 0, :], ref[:, :, E, :]
    y = lax.broadcasted_iota(jnp.int32, FACE, 2)
    ref[:, :, 0, :] = low + jnp.where(y > 0, pltpu.roll(high, 1, 2), 0.0)
    ref[:, :, E, :] = high + jnp.where(y < NY - 1, pltpu.roll(low, NY - 1, 2), 0.0)


def add_faces_x(ref, got, has, even):
    a, b = got[0][...], got[1][...]
    ref[0] = ref[0] + jnp.where(has[0], jnp.where(even[0], b, a), 0.0)
    ref[E] = ref[E] + jnp.where(has[1], jnp.where(even[0], a, b), 0.0)


def add_faces_z(ref, got, has, even):
    a, b = got[0][...], got[1][...]
    ref[:, 0] = ref[:, 0] + jnp.where(has[2], jnp.where(even[1], b, a), 0.0)
    ref[:, E] = ref[:, E] + jnp.where(has[3], jnp.where(even[1], a, b), 0.0)


def put_pair(even, low, high, out):
    out[0][...] = jnp.where(even, high, low)
    out[1][...] = jnp.where(even, low, high)


def aisle_stiffness(block):
    turned = jnp.swapaxes(block, 0, 1)
    out = apply1d([turned[c] for c in range(8)], K_)
    return jnp.swapaxes(jnp.stack(out, axis=0), 0, 1)


def local_operator(z_ref, f_ref, nb_ref, even, msgs):
    wk = kvec(W)
    kt, ct = nb_ref[4], nb_ref[13]
    kw, cw = kt * wk, ct * wk
    w0 = W[0]
    xc = {}
    for j in range(8):
        out = apply1d([z_ref[i, j] for i in range(8)], K_)
        kwj = kw * W[j]
        res = [kwj * out[i] for i in range(8)]
        for i in range(8):
            f_ref[i, j] = res[i]
        if j in (0, E):
            xc[0, j], xc[E, j] = out[0], out[E]
    for i in range(8):
        block = z_ref[i]
        v = [block[j] for j in range(8)]
        fx = [f_ref[i, j] for j in range(8)]
        zs = apply1d(v, K_)
        ys = aisle_stiffness(block)
        kwi = kw * W[i]
        res = [
            fx[j] + kwi * zs[j] + (W[i] * W[j]) * (kt * ys[j] + cw * v[j]) for j in range(8)
        ]
        for j in range(8):
            f_ref[i, j] = res[j]
        low, high = res[0], res[E]
        if i in (0, E):
            kn = nb_ref[1 if i == 0 else 7] * (w0 * wk)
            low, high = low + kn * zs[0], high + kn * zs[E]
            for j in (0, E):
                n = 3 if j == 0 else 5
                res[j] = (
                    res[j]
                    + nb_ref[n] * (w0 * wk * xc[i, j] + (w0 * w0) * ys[j])
                    + nb_ref[9 + n] * ((w0 * w0) * wk * v[j])
                )
            up, down = (1, 0) if i == 0 else (0, 1)

            @pl.when(even[0])
            def _(res=res, to=up):
                for j in range(8):
                    msgs[to][j] = res[j]

            @pl.when(jnp.logical_not(even[0]))
            def _(res=res, to=down):
                for j in range(8):
                    msgs[to][j] = res[j]

        msgs[2][i] = jnp.where(even[1], high, low)
        msgs[3][i] = jnp.where(even[1], low, high)


def thomas(cf_ref, rhs):
    dp = []
    for h in range(NZ):
        v = rhs[h] if h == 0 else rhs[h] - cf_ref[h] * dp[h - 1]
        dp.append(v * cf_ref[32 + h])
    for h in range(NZ - 2, -1, -1):
        dp[h] = dp[h] - cf_ref[16 + h] * dp[h + 1]
    return dp


def coarse_dot(a, b):
    acc = None
    for u, v in zip(a, b):
        acc = u * v if acc is None else acc + u * v
    return spread_sum(acc)


def spread_sum(tile):
    row = jnp.broadcast_to(jnp.sum(tile, axis=0, keepdims=True), (8, NY))
    return jnp.broadcast_to(jnp.sum(row, axis=1, keepdims=True), (8, NY))


def shift_pair(v, axis):
    n = v.shape[axis]
    p = lax.broadcasted_iota(jnp.int32, v.shape, axis)
    before = jnp.where(p == 0, v, pltpu.roll(v, 1, axis))
    after = jnp.where(p == n - 1, v, pltpu.roll(v, n - 1, axis))
    return before, after


def spread3(v, before, after):
    return (v, 0.5 * v + 0.25 * (before + after), 0.25 * (before - after))


def gather3(duals, axis):
    m, f, a = duals
    g, h = 0.25 * (f + a), 0.25 * (f - a)
    n = m.shape[axis]
    p = lax.broadcasted_iota(jnp.int32, m.shape, axis)
    up = jnp.where(p == n - 1, h, pltpu.roll(g, n - 1, axis))
    down = jnp.where(p == 0, g, pltpu.roll(h, 1, axis))
    return m + 0.5 * f + up + down


MU = (2.0 - 2.0 * W[0], 2.0 * W[0], 2.0 * W[0])
KS = float(2.0 * (K_[0, 0] + K_[0, 7]))
KA = float(2.0 * (K_[0, 0] - K_[0, 7]))


def stiff3(q):
    d = q[1] - q[0]
    return ((-KS / MU[0]) * d, (KS / MU[1]) * d, (KA / MU[2]) * q[2])


def coarse_operator(d, kc_ref, cc_ref, tmp_ref):
    for h in range(NZ):
        ys = spread3(d[h], *shift_pair(d[h], 1))
        for c in range(3):
            xs = spread3(ys[c], *shift_pair(ys[c], 0))
            for a in range(3):
                tmp_ref[(a * 3 + c) * NZ + h] = xs[a]
    part = []
    for h in range(NZ):
        lo, hi = max(h - 1, 0), min(h + 1, NZ - 1)
        q = {}
        for a in range(3):
            for c in range(3):
                base = (a * 3 + c) * NZ
                zs = spread3(tmp_ref[base + h], tmp_ref[base + lo], tmp_ref[base + hi])
                for b in range(3):
                    q[a, b, c] = zs[b]
        acc = {key: None for key in q}

        def add(key, val):
            acc[key] = val if acc[key] is None else acc[key] + val

        for b in range(3):
            for c in range(3):
                for n, val in enumerate(stiff3([q[a, b, c] for a in range(3)])):
                    add((n, b, c), val)
        for a in range(3):
            for c in range(3):
                for n, val in enumerate(stiff3([q[a, b, c] for b in range(3)])):
                    add((a, n, c), val)
        for a in range(3):
            for b in range(3):
                for n, val in enumerate(stiff3([q[a, b, c] for c in range(3)])):
                    add((a, b, n), val)
        kh, ch = kc_ref[h], cc_ref[h]
        outs = []
        for b in range(3):
            cols = []
            for c in range(3):
                duals = [
                    (MU[a] * MU[b] * MU[c]) * (kh * acc[a, b, c] + ch * q[a, b, c])
                    for a in range(3)
                ]
                cols.append(gather3(duals, 0))
            outs.append(gather3(cols, 1))
        part.append(outs)
    res = []
    for h in range(NZ):
        m, f, _ = part[h]
        v = m + 0.5 * f
        g = lambda n: 0.25 * (part[n][1] + part[n][2])
        l = lambda n: 0.25 * (part[n][1] - part[n][2])
        v = v + (g(h + 1) if h < NZ - 1 else l(h))
        v = v + (l(h - 1) if h > 0 else g(h))
        res.append(v)
    return res


def coarse_row(ref, ix, iz, dx, dz):
    x = jnp.clip(ix + dx, 0, NX - 1)
    z = jnp.clip(iz + dz, 0, NZ - 1)
    return ref[z, pl.ds(x, 1), :]


def aisle_tiles(row, want_stiff):
    c = jnp.broadcast_to(row, (8, NY))
    before, after = shift_pair(c, 1)
    k = lax.broadcasted_iota(jnp.int32, (8, NY), 0)
    low, high = 0.5 * (c + before), 0.5 * (c + after)
    tile = jnp.where(k == 0, low, jnp.where(k == E, high, c))
    if not want_stiff:
        return tile, None
    return tile, kvec(K_[:, 0]) * (low - c) + kvec(K_[:, 7]) * (high - c)


def classes(tiles, reach):
    n = 2 * reach + 1
    m = 2 * n - 3

    def line(vals):
        out = []
        for p in range(m):
            if p % 2 == 0:
                out.append(0.5 * (vals[p // 2] + vals[p // 2 + 1]))
            else:
                out.append(vals[p // 2 + 1])
        return out

    cols = [line(tiles[dx]) for dx in range(n)]
    by_q = [line([cols[dx][q] for dx in range(n)]) for q in range(m)]
    return [[by_q[q][p] for q in range(m)] for p in range(m)]


def cls(i):
    return 0 if i == 0 else (2 if i == E else 1)


def own_prolong(ref, ix, iz):
    tiles = [
        [aisle_tiles(coarse_row(ref, ix, iz, dx, dz), False)[0] for dz in (-1, 0, 1)]
        for dx in (-1, 0, 1)
    ]
    return classes(tiles, 1)


def add_operator_of_prolong(ref, ix, iz, nb_ref, out_ref):
    tv, ty = [], []
    for dx in range(-2, 3):
        pair = [aisle_tiles(coarse_row(ref, ix, iz, dx, dz), True) for dz in range(-2, 3)]
        tv.append([p[0] for p in pair])
        ty.append([p[1] for p in pair])
    v, yv = classes(tv, 2), classes(ty, 2)
    wk = kvec(W)

    def parts(ex, ez):
        p, q = 2 + 2 * ex, 2 + 2 * ez
        n = (ex + 1) * 3 + ez + 1
        kt, ct = nb_ref[n], nb_ref[9 + n]
        kw, cw = kt * wk, ct * wk
        memo = {}

        def once(key, make):
            if key not in memo:
                memo[key] = make()
            return memo[key]

        def along(i, a, b, c):
            return kw * (float(K_[i, 0]) * (a - b) + float(K_[i, 7]) * (c - b))

        def tile(i, j):
            a, b = cls(i), cls(j)
            xt = once(
                ("x", i, b), lambda: along(i, v[p][q + b], v[p + 1][q + b], v[p + 2][q + b])
            )
            zt = once(
                ("z", a, j), lambda: along(j, v[p + a][q], v[p + a][q + 1], v[p + a][q + 2])
            )
            yt = once(("y", a, b), lambda: kt * yv[p + a][q + b] + cw * v[p + a][q + b])
            return W[j] * xt + W[i] * zt + (W[i] * W[j]) * yt

        return tile

    part = {(ex, ez): parts(ex, ez) for ex in (-1, 0, 1) for ez in (-1, 0, 1)}
    for i in range(8):
        new = []
        for j in range(8):
            acc = out_ref[i, j] + part[0, 0](i, j)
            ex = -1 if i == 0 else (1 if i == E else 0)
            ez = -1 if j == 0 else (1 if j == E else 0)
            if ex:
                acc = acc + part[ex, 0](7 - i, j)
            if ez:
                acc = acc + part[0, ez](i, 7 - j)
            if ex and ez:
                acc = acc + part[ex, ez](7 - i, 7 - j)
            new.append(acc)
        for j in range(8):
            out_ref[i, j] = new[j]
    return [[v[2 + a][2 + b] for b in range(3)] for a in range(3)]


def make_z(c_ref, ix, iz, r_ref, dinv_ref, z_ref):
    pc = own_prolong(c_ref, ix, iz)
    for i in range(8):
        new = [r_ref[i, j] * dinv_ref[i, j] + pc[cls(i)][cls(j)] for j in range(8)]
        for j in range(8):
            z_ref[i, j] = new[j]


def coarse_rows_of(got_ref, which):
    return [got_ref[pl.ds(4 * h + which, NX, stride=4 * NZ), :] for h in range(NZ)]


def heat_kernel(pos, heat, cond, marks, f, ma, mb, kc, mk, buf, sems):
    copies = [
        pltpu.make_async_copy(src, dst, sems.at[n])
        for n, (src, dst) in enumerate(((heat, buf), (cond, kc), (marks, mk)))
    ]
    for copy in copies:
        copy.start()
    _, _, _, _, even = place(pos)
    wk = kvec(W)
    for copy in copies:
        copy.wait()
    for i in range(8):
        new = [(W[i] * W[j]) * wk * buf[i, j] for j in range(8)]
        for j in range(8):
            f[i, j] = new[j]
    put_pair(even[0], f[0], f[E], (ma, mb))


def heat_z_kernel(pos, f, ra, rb, out, ma, mb):
    _, _, has, _, even = place(pos)
    out[...] = f[...]
    add_faces_x(out, (ra, rb), has, even)
    put_pair(even[1], out[:, 0], out[:, E], (ma, mb))


def first_rows_kernel(pos, f, ra, rb, kc, marks, out, rows):
    _, _, has, frac, even = place(pos)
    out[...] = f[...]
    add_faces_z(out, (ra, rb), has, even)
    assemble_aisle(out)
    tile = field_sum(lambda i, j: out[i, j], frac) * own_mult()
    restricted = jnp.sum(tile, axis=0, keepdims=True)
    cap = jnp.where(marks[...] == 1, jnp.float32(HEAT_SOLID), jnp.float32(HEAT_AIR))
    block = jnp.concatenate([kc[...], cap, restricted, jnp.zeros((1, NY), F32)], axis=0)
    rows[...] = jnp.broadcast_to(block[None], rows.shape)


def setup_kernel(
    pos, got, r, kc, cc, cf, rc, nb, dinv, z, f, m0, m1, m2, m3, c_tmp
):
    ix, iz, has, frac, even = place(pos)
    k_all, c_all, r_all = (coarse_rows_of(got, n) for n in range(3))
    for h in range(NZ):
        kc[h], cc[h], rc[h] = k_all[h], c_all[h], r_all[h]
    link = [2.0 * k_all[h] * k_all[h + 1] / (k_all[h] + k_all[h + 1]) for h in range(NZ - 1)]
    above = None
    for h in range(NZ):
        main = 8.0 * c_all[h]
        if h > 0:
            main = main + link[h - 1]
        if h < NZ - 1:
            main = main + link[h]
        low = -link[h - 1] if h > 0 else jnp.zeros((NX, NY), F32)
        piv = main if h == 0 else main - low * above
        inv = 1.0 / piv
        above = -link[h] * inv if h < NZ - 1 else jnp.zeros((NX, NY), F32)
        cf[h], cf[16 + h], cf[32 + h] = low, above, inv
    for ex in (-1, 0, 1):
        for ez in (-1, 0, 1):
            n = (ex + 1) * 3 + ez + 1
            there = None
            if ex:
                there = has[0] if ex < 0 else has[1]
            if ez:
                hz = has[2] if ez < 0 else has[3]
                there = hz if there is None else there & hz
            for base, src in ((0, kc), (9, cc)):
                tile = jnp.broadcast_to(coarse_row(src, ix, iz, ex, ez), (8, NY))
                nb[base + n] = tile if there is None else jnp.where(there, tile, 0.0)
    wk, sk = kvec(W), kvec(SD)
    for i in range(8):
        for j in range(8):
            ex = -1 if i == 0 else (1 if i == E else 0)
            ez = -1 if j == 0 else (1 if j == E else 0)
            kt, ct = nb[4], nb[13]
            for n in {4 + 3 * ex, 4 + ez, 4 + 3 * ex + ez} - {4}:
                kt, ct = kt + nb[n], ct + nb[9 + n]
            dinv[i, j] = (
                kt * ((SD[i] * W[j] + W[i] * SD[j]) * wk + (W[i] * W[j]) * sk)
                + ct * ((W[i] * W[j]) * wk)
            )
    assemble_aisle(dinv)
    dinv[...] = 1.0 / dinv[...]
    solved = thomas(cf, r_all)
    for h in range(NZ):
        c_tmp[h] = solved[h]
    make_z(c_tmp, ix, iz, r, dinv, z)
    local_operator(z, f, nb, even, (m0, m1, m2, m3))


def inner_kernel(pos, f, r0, r1, r2, r3, nb, dinv, *refs):
    w1, t, f2, m0, m1, m2, m3 = refs[-7:]
    _, _, has, _, even = place(pos)
    w1[...] = f[...]
    add_faces_x(w1, (r0, r1), has, even)
    add_faces_z(w1, (r2, r3), has, even)
    assemble_aisle(w1)
    t[...] = w1[...] * dinv[...]
    local_operator(t, f2, nb, even, (m0, m1, m2, m3))


def dots_kernel(first, *refs):
    if first:
        pos, z, r, t, w1, lines = refs
    else:
        pos, z, r, t, w1, s1, s2, lines = refs
    _, _, _, frac, _ = place(pos)
    my = own_mult()
    zero = jnp.zeros((1, NY), F32)

    def dot(a, b):
        tile = my * field_sum(lambda i, j: a[i, j] * b[i, j], frac)
        return jnp.sum(tile, axis=0, keepdims=True)

    out = [dot(z, r), dot(t, r), dot(z, w1), dot(t, w1), zero]
    out += [zero] * 4 if first else [dot(z, s1), dot(z, s2), dot(t, s1), dot(t, s2)]
    out += [zero] * 6
    out.append(jnp.sum(field_sum(lambda i, j: w1[i, j], frac) * my, axis=0, keepdims=True))
    lines[...] = jnp.concatenate(out, axis=0)


def rows_kernel(first, *refs):
    if first:
        pos, f2, r0, r1, r2, r3, t, lines, owners, v, rows = refs
    else:
        pos, f2, r0, r1, r2, r3, t, lines, v, rows = refs
    _, _, has, frac, even = place(pos)
    v[...] = f2[...]
    add_faces_x(v, (r0, r1), has, even)
    add_faces_z(v, (r2, r3), has, even)
    my = own_mult()
    tv = jnp.sum(field_sum(lambda i, j: t[i, j] * v[i, j], frac), axis=0, keepdims=True)
    lane = lax.broadcasted_iota(jnp.int32, (16, NY), 1)
    at = lax.broadcasted_iota(jnp.int32, (16, NY), 0)
    stacked = jnp.where(at == 4, jnp.broadcast_to(tv, (16, NY)), lines[...])
    totals = jnp.broadcast_to(jnp.sum(stacked, axis=1, keepdims=True), (16, NY))
    dots = jnp.sum(jnp.where(lane == at, totals, 0.0), axis=0, keepdims=True)
    vt = field_sum(lambda i, j: v[i, j], frac)
    k = lax.broadcasted_iota(jnp.int32, (8, NY), 0)
    y = lax.broadcasted_iota(jnp.int32, (8, NY), 1)
    vlow = jnp.broadcast_to(vt[0:1], (8, NY))
    vhigh = jnp.broadcast_to(vt[7:8], (8, NY))
    vt = vt + jnp.where((k == 0) & (y > 0), pltpu.roll(vhigh, 1, 1), 0.0)
    vt = vt + jnp.where((k == E) & (y < NY - 1), pltpu.roll(vlow, NY - 1, 1), 0.0)
    g2 = jnp.sum(vt * my, axis=0, keepdims=True)
    block = jnp.concatenate([lines[15:16], g2, dots, jnp.zeros((1, NY), F32)], axis=0)
    rows[...] = jnp.broadcast_to(block[None], rows.shape)
    if first:
        rows[:, 3, :] = owners[...]


def coefficients(first, got, d, q, rc, rs, wp, cf):
    total = got[0:8]
    for n in range(8, NX * NZ * 4, 8):
        total = total + got[n : n + 8]
    dots = jnp.broadcast_to(total[2:3] + total[6:7], (8, NY))
    lane = lax.broadcasted_iota(jnp.int32, (8, NY), 1)

    def pick(n):
        return jnp.broadcast_to(
            jnp.sum(jnp.where(lane == n, dots, 0.0), axis=1, keepdims=True), (8, NY)
        )

    g1, g2 = coarse_rows_of(got, 0), coarse_rows_of(got, 1)
    b1, b2 = pick(0), pick(1) + coarse_dot(d, [rc[h] for h in range(NZ)])
    w11 = pick(2)
    w12 = pick(3) + coarse_dot(d, g1)
    w22 = pick(4) + 2.0 * coarse_dot(d, g2) + coarse_dot(d, q)
    e = [None] * 4
    if not first:
        rs1, rs2 = [rs[h] for h in range(NZ)], [rs[NZ + h] for h in range(NZ)]
        c11, c21 = pick(5), pick(6)
        c12, c22 = pick(7) + coarse_dot(d, rs1), pick(8) + coarse_dot(d, rs2)
        pa, pb, pc = wp[6], wp[7], wp[8]
        inv = -1.0 / (pa * pc - pb * pb)
        e11, e21 = (pc * c11 - pb * c21) * inv, (pa * c21 - pb * c11) * inv
        e12, e22 = (pc * c12 - pb * c22) * inv, (pa * c22 - pb * c12) * inv
        w11 = w11 + c11 * e11 + c21 * e21
        w12 = w12 + c11 * e12 + c21 * e22
        w22 = w22 + c12 * e12 + c22 * e22
        e = [e11, e21, e12, e22]
    inv = 1.0 / (w11 * w22 - w12 * w12)
    a1 = (w22 * b1 - w12 * b2) * inv
    a2 = (w11 * b2 - w12 * b1) * inv
    return a1, a2, e, (w11, w12, w22), g1, g2


def new_residual(first, a1, a2, x1, x2, r, w1, ay, s1, s2, out):
    for i in range(8):
        new = []
        for j in range(8):
            v = r[i, j] - (a1 * w1[i, j] + a2 * ay[i, j])
            if not first:
                v = v - (x1 * s1[i, j] + x2 * s2[i, j])
            new.append(v)
        for j in range(8):
            out[i, j] = new[j]


def step_kernel(first, *refs):
    refs = list(refs)
    take = lambda n: [refs.pop(0) for _ in range(n)]
    pos, got, r, w1, v, dinv, nb, kc, cc, cf, rc = take(11)
    s1 = s2 = rs = wp = None
    if not first:
        s1, s2, rs, wp = take(4)
    ro, rco, zo, fo, m0, m1, m2, m3, co, ay, pdo, qo = take(12)
    c_tmp, tmp = take(2)
    ix, iz, has, frac, even = place(pos)
    d = thomas(cf, coarse_rows_of(got, 0))
    for h in range(NZ):
        c_tmp[h] = d[h]
    q = coarse_operator(d, kc, cc, tmp)
    a1, a2, e, w, g1, g2 = coefficients(first, got, d, q, rc, rs, wp, cf)
    x1 = x2 = None
    if not first:
        x1, x2 = a1 * e[0] + a2 * e[2], a1 * e[1] + a2 * e[3]
    for n, val in enumerate((a1, a2, *e, *w)):
        if val is not None:
            co[n] = val
        else:
            co[n] = jnp.zeros((8, NY), F32)
    ay[...] = v[...]
    pd = add_operator_of_prolong(c_tmp, ix, iz, nb, ay)
    for n in range(9):
        pdo[n] = pd[n // 3][n % 3]
    assemble_aisle(ay)
    new_residual(first, a1, a2, x1, x2, r, w1, ay, s1, s2, ro)
    rnew = []
    for h in range(NZ):
        qo[h] = q[h]
        new = rc[h] - (a1 * g1[h] + a2 * (g2[h] + q[h]))
        if not first:
            new = new - (x1 * rs[h] + x2 * rs[NZ + h])
        rco[h] = new
        rnew.append(new)
    solved = thomas(cf, rnew)
    for h in range(NZ):
        c_tmp[h] = solved[h]
    make_z(c_tmp, ix, iz, ro, dinv, zo)
    local_operator(zo, fo, nb, even, (m0, m1, m2, m3))


def new_x(first, a1, a2, x1, x2, z, t, pd, p1, p2, x, out):
    for i in range(8):
        new = []
        for j in range(8):
            up = a1 * z[i, j] + a2 * (t[i, j] + pd(i, j))
            if not first:
                up = x[i, j] + (up + (x1 * p1[i, j] + x2 * p2[i, j]))
            new.append(up)
        for j in range(8):
            out[i, j] = new[j]


def late_kernel(first, *refs):
    refs = list(refs)
    take = lambda n: [refs.pop(0) for _ in range(n)]
    got, z, t, w1, ay, co, pdt, q = take(8)
    x = p1 = p2 = s1 = s2 = rs = None
    if not first:
        x, p1, p2, s1, s2, rs = take(6)
    xo, p1o, p2o, s1o, s2o, rso = take(6)
    a1, a2, e11, e21, e12, e22 = (co[n] for n in range(6))
    x1, x2 = a1 * e11 + a2 * e12, a1 * e21 + a2 * e22
    pd = lambda i, j: pdt[3 * cls(i) + cls(j)]
    new_x(first, a1, a2, x1, x2, z, t, pd, p1, p2, x, xo)

    def block(one, two, prev1, prev2, out1, out2):
        for i in range(8):
            new = []
            for j in range(8):
                n1, n2 = one(i, j), two(i, j)
                if not first:
                    u, w = prev1[i, j], prev2[i, j]
                    n1, n2 = n1 + e11 * u + e21 * w, n2 + e12 * u + e22 * w
                new.append((n1, n2))
            for j in range(8):
                out1[i, j], out2[i, j] = new[j]

    block(lambda i, j: z[i, j], lambda i, j: t[i, j] + pd(i, j), p1, p2, p1o, p2o)
    block(lambda i, j: w1[i, j], lambda i, j: ay[i, j], s1, s2, s1o, s2o)
    g1, g2 = coarse_rows_of(got, 0), coarse_rows_of(got, 1)
    for h in range(NZ):
        n1, n2 = g1[h], g2[h] + q[h]
        if not first:
            u, w = rs[h], rs[NZ + h]
            n1, n2 = n1 + e11 * u + e21 * w, n2 + e12 * u + e22 * w
        rso[h], rso[NZ + h] = n1, n2


def last_kernel(pos, got, z, t, nb, kc, cc, cf, rc, x, p1, p2, rs, wp, table, xo, send, co, dc, tmp):
    ix, iz, _, _, _ = place(pos)
    d = thomas(cf, coarse_rows_of(got, 0))
    for h in range(NZ):
        dc[h] = d[h]
    q = coarse_operator(d, kc, cc, tmp)
    a1, a2, e, _, _, _ = coefficients(False, got, d, q, rc, rs, wp, cf)
    x1, x2 = a1 * e[0] + a2 * e[2], a1 * e[1] + a2 * e[3]
    for n, val in enumerate((a1, a2, x1, x2)):
        co[n] = val
    own = own_prolong(dc, ix, iz)
    pd = lambda i, j: own[cls(i)][cls(j)]
    new_x(False, a1, a2, x1, x2, z, t, pd, p1, p2, x, xo)
    put_rows(xo, nb, table, send)


def residual_kernel(pos, co, dc, v, r, w1, s1, s2, nb, ro, ay):
    ix, iz, _, _, _ = place(pos)
    ay[...] = v[...]
    add_operator_of_prolong(dc, ix, iz, nb, ay)
    assemble_aisle(ay)
    new_residual(False, co[0], co[1], co[2], co[3], r, w1, ay, s1, s2, ro)


NT = (((1,), (1,)), ((), ()))
SLOTS = 16


def slots_kernel(own_in, elem_in, side_in, target_in, table, owners, own, elem, side, target, sems):
    pairs = ((own_in, own), (elem_in, elem), (side_in, side), (target_in, target))
    copies = [pltpu.make_async_copy(src, dst, sems.at[n]) for n, (src, dst) in enumerate(pairs)]
    for copy in copies:
        copy.start()
    for copy in copies:
        copy.wait()
    faces = own.shape[1]
    row = own[...].astype(F32)
    col = jnp.broadcast_to(row, (NY, faces)).T
    ranks = []
    for s in range(0, faces, NY):
        f = lax.broadcasted_iota(jnp.int32, (faces, NY), 0)
        g = lax.broadcasted_iota(jnp.int32, (faces, NY), 1) + s
        same = (col == row[:, s : s + NY]) & (f < g)
        ranks.append(jnp.sum(jnp.where(same, 1.0, 0.0), axis=0, keepdims=True))
    rank = jnp.concatenate(ranks, axis=1)
    slot = row * SLOTS + rank
    vals = jnp.concatenate(
        [elem[...].astype(F32) + 1.0, side[...].astype(F32), jnp.zeros((6, faces), F32)], axis=0
    ).astype(jnp.bfloat16)
    step = 256
    for s in range(0, table.shape[0], step):
        at = lax.broadcasted_iota(jnp.int32, (step, faces), 0).astype(F32) + float(s)
        hot = jnp.where(at == slot, 1.0, 0.0).astype(jnp.bfloat16)
        got = lax.dot_general(hot, vals, NT, preferred_element_type=F32)
        pick = got[:, 0:1] - 1.0 + 128.0 * got[:, 1:2]
        lane = lax.broadcasted_iota(jnp.int32, (step, table.shape[1]), 1).astype(F32)
        table[s : s + step] = jnp.where(lane == pick, 1.0, 0.0).astype(jnp.bfloat16)
    devices = owners.shape[0]
    dev = lax.broadcasted_iota(jnp.int32, (devices, faces), 0).astype(F32)
    hot = jnp.where(dev == row, 1.0, 0.0).astype(jnp.bfloat16)
    at = lax.broadcasted_iota(jnp.int32, (128, faces), 0).astype(F32)
    marked = jnp.where(at == rank, target[...].astype(F32) + 1.0, 0.0).astype(jnp.bfloat16)
    owners[...] = lax.dot_general(hot, marked, NT, preferred_element_type=F32) - 1.0


def owners_kernel(got, hot_t):
    devices = got.shape[0] // 4
    lane = lax.broadcasted_iota(jnp.int32, (SLOTS, NY), 1)
    at = lax.broadcasted_iota(jnp.int32, (SLOTS, NY), 0)
    ones = jnp.ones((NY, NY), jnp.bfloat16)
    step = 8
    for d in range(0, devices, step):
        rows = [
            jnp.where(lane == at, jnp.broadcast_to(got[4 * (d + n) + 3 : 4 * (d + n) + 4], (SLOTS, NY)), 0.0)
            for n in range(step)
        ]
        block = jnp.concatenate(rows, axis=0).astype(jnp.bfloat16)
        col = jnp.dot(block, ones, preferred_element_type=F32)
        elem = lax.broadcasted_iota(jnp.int32, col.shape, 1).astype(F32)
        hot = jnp.where(col == elem, 1.0, 0.0)
        hot_t[:, d * SLOTS : (d + step) * SLOTS] = hot.T.astype(jnp.bfloat16)


def split(v):
    high = v.astype(jnp.bfloat16)
    return high, (v - high.astype(F32)).astype(jnp.bfloat16)


def put_rows(x, nb, table, send):
    kt = nb[4]

    def weighted(get, row):
        acc = None
        for a in range(8):
            term = float(D_[row, a]) * get(a)
            acc = term if acc is None else acc + term
        return acc

    getters = (lambda a: x[a], lambda a: x[:, a], lambda a: x[:, :, a, :])
    his, los = [], []
    for get in getters:
        for end, sign in ((0, 1.0), (E, -1.0)):
            flux = weighted(get, end) * (sign * kt)[None]
            block = jnp.concatenate(
                [flux.reshape(64, NY), get(end).reshape(64, NY)], axis=0
            )
            h, l = split(block)
            his.append(h)
            los.append(l)
    both = jnp.concatenate(
        [jnp.concatenate(his, axis=1), jnp.concatenate(los, axis=1)], axis=0
    )
    step = 512
    for s in range(0, send.shape[0], step):
        out = lax.dot_general(table[s : s + step], both, NT, preferred_element_type=F32)
        send[s : s + step] = out[:, :NY] + out[:, NY:]


def load_kernel(got, hot_t, out):
    acc = None
    step = 512
    for s in range(0, got.shape[0], step):
        hi, lo = split(got[s : s + step])
        hot = hot_t[:, s : s + step]
        term = jnp.dot(hot, hi, preferred_element_type=F32) + jnp.dot(
            hot, lo, preferred_element_type=F32
        )
        acc = term if acc is None else acc + term
    out[...] = acc.T


def call(body, name, outs, args, scratch=(), copied=()):
    vmem = pl.BlockSpec(memory_space=pltpu.VMEM)
    shape = lambda o: o if isinstance(o[0], tuple) else (o, F32)

    def spec(n, a):
        if n in copied:
            return pl.BlockSpec(memory_space=pltpu.HBM)
        if a.dtype == jnp.int32 and a.shape == (2,):
            return pl.BlockSpec(memory_space=pltpu.SMEM)
        return vmem

    return pl.pallas_call(
        body,
        out_shape=[jax.ShapeDtypeStruct(*shape(o)) for o in outs],
        in_specs=[spec(n, a) for n, a in enumerate(args)],
        out_specs=[vmem] * len(outs),
        scratch_shapes=[pltpu.VMEM(*shape(s)) if isinstance(s, tuple) else s for s in scratch],
        compiler_params=pltpu.CompilerParams(vmem_limit_bytes=24 * 1024 * 1024),
        cost_estimate=pl.CostEstimate(
            flops=2_000_000, bytes_accessed=1 << 20, transcendentals=0
        ),
        name=name,
    )(*args)


def pair_perms(n):
    first = [(i, i ^ 1) for i in range(n)]
    second = [(i, (i + 1) % n if i % 2 else (i - 1) % n) for i in range(n)]
    return first, second


def swap_x(pair):
    a, b = pair_perms(NX)
    return [lax.ppermute(pair[0], "row", a), lax.ppermute(pair[1], "row", b)]


def swap_z(pair):
    a, b = pair_perms(NZ)
    return [lax.ppermute(pair[0], "height", a), lax.ppermute(pair[1], "height", b)]


def everywhere(rows):
    return lax.all_to_all(rows, ("row", "height"), split_axis=0, concat_axis=0, tiled=True)


def shards(heat, conductivity, marks, face_owner, face_element, face_side, owner_element):
    devices = NX * NZ
    pos = jnp.stack([lax.axis_index("row"), lax.axis_index("height")]).astype(jnp.int32)
    row = lambda a: a.reshape(1, -1)
    line = ((1, NY), F32)
    faces = ((1, face_element.shape[0]), jnp.int32)
    f, ma, mb, cond, marks = call(
        heat_kernel,
        "heat",
        [FIELD, FACE, FACE, line, ((1, NY), jnp.int32)],
        [pos, heat.reshape(FIELD), row(conductivity), row(marks)],
        scratch=[FIELD, pltpu.SemaphoreType.DMA((3,))],
        copied=(1, 2, 3),
    )
    ra, rb = swap_x((ma, mb))
    table, owners = call(
        slots_kernel,
        "slots",
        [((devices * SLOTS, 6 * NY), jnp.bfloat16), (devices, 128)],
        [row(face_owner), row(face_element), row(face_side), row(owner_element)],
        scratch=[faces] * 4 + [pltpu.SemaphoreType.DMA((4,))],
        copied=(0, 1, 2, 3),
    )
    f, ma, mb = call(heat_z_kernel, "heat_z", [FIELD, FACE, FACE], [pos, f, ra, rb])
    ra, rb = swap_z((ma, mb))
    r, rows = call(
        first_rows_kernel,
        "first_rows",
        [FIELD, (devices, 4, NY)],
        [pos, f, ra, rb, cond, marks],
    )
    got0 = everywhere(rows).reshape(devices * 4, NY)
    kc, cc, cf, rc, nb, dinv, z, f, *msgs = call(
        setup_kernel,
        "setup",
        [COARSE, COARSE, (48, NX, NY), COARSE, (18, 8, NY), FIELD, FIELD, FIELD] + [FACE] * 4,
        [pos, got0, r],
        scratch=[COARSE],
    )
    x = p1 = p2 = s1 = s2 = rs = co = None
    for outer in range(ITERS // 2):
        first, last = outer == 0, outer == ITERS // 2 - 1
        got = swap_x(msgs[:2]) + swap_z(msgs[2:])
        w1, t, f2, *msgs = call(
            inner_kernel,
            "inner",
            [FIELD] * 3 + [FACE] * 4,
            [pos, f, *got, nb, dinv] + ([] if first else [rs]),
        )
        got = swap_x(msgs[:2]) + swap_z(msgs[2:])
        (lines,) = call(
            functools.partial(dots_kernel, first),
            "dots",
            [(16, NY)],
            [pos, z, r, t, w1] + ([] if first else [s1, s2]),
        )
        v, rows = call(
            functools.partial(rows_kernel, first),
            "rows",
            [FIELD, (devices, 4, NY)],
            [pos, f2, *got, t, lines] + ([owners] if first else []),
        )
        rows = everywhere(rows).reshape(devices * 4, NY)
        if first:
            (hot_t,) = call(
                owners_kernel, "owners", [((NY, devices * SLOTS), jnp.bfloat16)], [rows]
            )
        if last:
            break
        rn, rcn, zn, f, *msgs, con, ay, pd, q = call(
            functools.partial(step_kernel, first),
            "step",
            [FIELD, COARSE, FIELD, FIELD]
            + [FACE] * 4
            + [(9, 8, NY), FIELD, (9, 8, NY), COARSE],
            [pos, rows, r, w1, v, dinv, nb, kc, cc, cf, rc] + ([] if first else [s1, s2, rs, co]),
            scratch=[COARSE, (9 * NZ, NX, NY)],
        )
        x, p1, p2, s1, s2, rs = call(
            functools.partial(late_kernel, first),
            "late",
            [FIELD] * 5 + [(2 * NZ, NX, NY)],
            [rows, z, t, w1, ay, con, pd, q] + ([] if first else [x, p1, p2, s1, s2, rs]),
        )
        r, rc, z, co = rn, rcn, zn, con
    x, send, coef, d = call(
        last_kernel,
        "last",
        [FIELD, (devices * SLOTS, NY), (4, 8, NY), COARSE],
        [pos, rows, z, t, nb, kc, cc, cf, rc, x, p1, p2, rs, co, table],
        scratch=[(9 * NZ, NX, NY)],
    )
    got = everywhere(send.reshape(devices, SLOTS, NY))
    (r,) = call(
        residual_kernel,
        "residual",
        [FIELD],
        [pos, coef, d, v, r, w1, s1, s2, nb],
        scratch=[FIELD],
    )
    (load,) = call(
        load_kernel, "load", [(NY, NY)], [got.reshape(devices * SLOTS, NY), hot_t]
    )
    shape = (8, 8, 8, 1, 1, NY)
    return (x.reshape(shape), r.reshape(shape), load.reshape(NY, 1, 1, NY))


def solution(mesh):
    in_specs = (
        P(None, None, None, "row", "height", None),
        P("row", "height", None),
        P("row", "height", None),
        P(("row", "height"), None),
        P(("row", "height")),
        P(("row", "height")),
        P(("row", "height")),
    )
    out_specs = (
        P(None, None, None, "row", "height", None),
        P(None, None, None, "row", "height", None),
        P(None, "row", "height", None),
    )
    return jax.shard_map(shards, mesh=mesh, in_specs=in_specs, out_specs=out_specs, check_vma=False)
```

profile of v0, /device:TPU:1, one launch (start us, length us, event | category | flops | bytes accessed | tf_op | source)
XLA Modules:
  0.0 218.6 jit_solution(7666944582008854947)
XLA Ops:
  10.4 4.3 %collective-permute-start.3 = (f32[8,8,128]{2,1,0:T(8,128)S(1)}, f32[8,8,128]{2,1,0:T(8,128)S(1)}, u32[]{:S(2)}, u32[]{:S(2)}) collective-permute-start(f32[8,8,128]{2,1,0:T(8,128)S(1)} %get-tuple-element.126), channel_id=1, source_target_pairs={{0,15},{1,2},{2,1},{3,4},{4,3},{5,6},{6,5},{7,8},{8,7},{9,10},{10,... | collective-permute-start | bytes 98312 | tf_op jit(solution)/shard_map/ppermute | solution.py:890
  14.7 1.8 collective-permute-done.3.rb
  17.2 21.5 %all_to_all.30 = f32[128,4,128]{2,1,0:T(4,128)S(1)} all-to-all(f32[128,4,128]{2,1,0:T(4,128)S(1)} %get-tuple-element.129), channel_id=1, replica_groups=mesh['row'=8,'height'=16] {'row','height'}, dimensions={0} | all-to-all | bytes 524288 | tf_op jit(solution)/shard_map/all_to_all | solution.py:894
  44.3 3.6 %collective-permute-done.7.r3 = f32[8,8,128]{2,1,0:T(8,128)S(1)} collective-permute-done((f32[8,8,128]{2,1,0:T(8,128)S(1)}, f32[8,8,128]{2,1,0:T(8,128)S(1)}, u32[]{:S(2)}, u32[]{:S(2)}) %collective-permute-start.7) | collective-permute-done | bytes 32800 | tf_op jit(solution)/shard_map/ppermute | solution.py:890
  50.1 2.2 %collective-permute-start.8 = (f32[8,8,128]{2,1,0:T(8,128)S(1)}, f32[8,8,128]{2,1,0:T(8,128)S(1)}, u32[]{:S(2)}, u32[]{:S(2)}) collective-permute-start(f32[8,8,128]{2,1,0:T(8,128)S(1)} %get-tuple-element.139), channel_id=1, source_target_pairs={{0,16},{16,0},{32,48},{48,32},{64,80},{80,64},{96,112},{112,96},{1... | collective-permute-start | bytes 98312 | tf_op jit(solution)/shard_map/ppermute | solution.py:885
  59.0 17.9 %all_to_all.31 = f32[128,4,128]{2,1,0:T(4,128)S(1)} all-to-all(f32[128,4,128]{2,1,0:T(4,128)S(1)} %get-tuple-element.147), channel_id=1, replica_groups=mesh['row'=8,'height'=16] {'row','height'}, dimensions={0} | all-to-all | bytes 524288 | tf_op jit(solution)/shard_map/all_to_all | solution.py:894
  76.9 2.8 %step.3 = (f32[8,8,8,128]{3,2,1,0:T(8,128)S(1)}, f32[16,8,128]{2,1,0:T(8,128)S(1)}, f32[8,8,8,128]{3,2,1,0:T(8,128)S(1)}, f32[8,8,8,128]{3,2,1,0:T(8,128)S(1)}, ...) custom-call(s32[2]{0:T(128)S(1)} %pad_add_fusion.pos.refs_0_, ...), custom_call_target="tpu_custom_call" | custom-call | flops 2000000 | bytes 1048576 | tf_op jit(solution)/shard_map/step/pallas_call | solution.py:863
  83.8 3.6 %collective-permute-done.15.r3 = f32[8,8,128]{2,1,0:T(8,128)S(1)} collective-permute-done((f32[8,8,128]{2,1,0:T(8,128)S(1)}, f32[8,8,128]{2,1,0:T(8,128)S(1)}, u32[]{:S(2)}, u32[]{:S(2)}) %collective-permute-start.15) | collective-permute-done | bytes 32800 | tf_op jit(solution)/shard_map/ppermute | solution.py:890
  88.5 2.0 collective-permute-start.16
  94.4 3.3 %collective-permute-done.19.refs_5_ = f32[8,8,128]{2,1,0:T(8,128)S(1)} collective-permute-done((f32[8,8,128]{2,1,0:T(8,128)S(1)}, f32[8,8,128]{2,1,0:T(8,128)S(1)}, u32[]{:S(2)}, u32[]{:S(2)}) %collective-permute-start.19) | collective-permute-done | bytes 32800 | tf_op jit(solution)/shard_map/ppermute | solution.py:890
  98.5 16.1 %all_to_all.32 = f32[128,4,128]{2,1,0:T(4,128)S(1)} all-to-all(f32[128,4,128]{2,1,0:T(4,128)S(1)} %get-tuple-element.174), channel_id=1, replica_groups=mesh['row'=8,'height'=16] {'row','height'}, dimensions={0} | all-to-all | bytes 524288 | tf_op jit(solution)/shard_map/all_to_all | solution.py:894
  114.6 2.8 %step.4 = (f32[8,8,8,128]{3,2,1,0:T(8,128)S(1)}, f32[16,8,128]{2,1,0:T(8,128)S(1)}, f32[8,8,8,128]{3,2,1,0:T(8,128)S(1)}, f32[8,8,8,128]{3,2,1,0:T(8,128)S(1)}, ...) custom-call(s32[2]{0:T(128)S(1)} %pad_add_fusion.pos.refs_0_, ...), custom_call_target="tpu_custom_call" | custom-call | flops 2000000 | bytes 1048576 | tf_op jit(solution)/shard_map/step/pallas_call | solution.py:863
  121.5 3.6 %collective-permute-done.23.r3 = f32[8,8,128]{2,1,0:T(8,128)S(1)} collective-permute-done((f32[8,8,128]{2,1,0:T(8,128)S(1)}, f32[8,8,128]{2,1,0:T(8,128)S(1)}, u32[]{:S(2)}, u32[]{:S(2)}) %collective-permute-start.23) | collective-permute-done | bytes 32800 | tf_op jit(solution)/shard_map/ppermute | solution.py:890
  126.3 2.0 collective-permute-start.24
  132.2 3.3 %collective-permute-done.27.refs_5_ = f32[8,8,128]{2,1,0:T(8,128)S(1)} collective-permute-done((f32[8,8,128]{2,1,0:T(8,128)S(1)}, f32[8,8,128]{2,1,0:T(8,128)S(1)}, u32[]{:S(2)}, u32[]{:S(2)}) %collective-permute-start.27) | collective-permute-done | bytes 32800 | tf_op jit(solution)/shard_map/ppermute | solution.py:890
  136.2 16.1 %all_to_all.33 = f32[128,4,128]{2,1,0:T(4,128)S(1)} all-to-all(f32[128,4,128]{2,1,0:T(4,128)S(1)} %get-tuple-element.201), channel_id=1, replica_groups=mesh['row'=8,'height'=16] {'row','height'}, dimensions={0} | all-to-all | bytes 524288 | tf_op jit(solution)/shard_map/all_to_all | solution.py:894
  152.3 2.8 %step.5 = (f32[8,8,8,128]{3,2,1,0:T(8,128)S(1)}, f32[16,8,128]{2,1,0:T(8,128)S(1)}, f32[8,8,8,128]{3,2,1,0:T(8,128)S(1)}, f32[8,8,8,128]{3,2,1,0:T(8,128)S(1)}, ...) custom-call(s32[2]{0:T(128)S(1)} %pad_add_fusion.pos.refs_0_, ...), custom_call_target="tpu_custom_call" | custom-call | flops 2000000 | bytes 1048576 | tf_op jit(solution)/shard_map/step/pallas_call | solution.py:863
  159.5 3.6 %collective-permute-done.31.r3 = f32[8,8,128]{2,1,0:T(8,128)S(1)} collective-permute-done((f32[8,8,128]{2,1,0:T(8,128)S(1)}, f32[8,8,128]{2,1,0:T(8,128)S(1)}, u32[]{:S(2)}, u32[]{:S(2)}) %collective-permute-start.31) | collective-permute-done | bytes 32800 | tf_op jit(solution)/shard_map/ppermute | solution.py:890
  164.2 1.8 collective-permute-start.32
  169.9 3.0 %collective-permute-done.35.refs_5_ = f32[8,8,128]{2,1,0:T(8,128)S(1)} collective-permute-done((f32[8,8,128]{2,1,0:T(8,128)S(1)}, f32[8,8,128]{2,1,0:T(8,128)S(1)}, u32[]{:S(2)}, u32[]{:S(2)}) %collective-permute-start.35) | collective-permute-done | bytes 32800 | tf_op jit(solution)/shard_map/ppermute | solution.py:890
  173.7 16.4 %all_to_all.34 = f32[128,4,128]{2,1,0:T(4,128)S(1)} all-to-all(f32[128,4,128]{2,1,0:T(4,128)S(1)} %get-tuple-element.228), channel_id=1, replica_groups=mesh['row'=8,'height'=16] {'row','height'}, dimensions={0} | all-to-all | bytes 524288 | tf_op jit(solution)/shard_map/all_to_all | solution.py:894
  190.1 4.3 %last.1 = (f32[8,8,8,128]{3,2,1,0:T(8,128)}, f32[2048,128]{1,0:T(8,128)}, f32[4,8,128]{2,1,0:T(8,128)S(1)}, f32[16,8,128]{2,1,0:T(8,128)S(1)}) custom-call(s32[2]{0:T(128)S(1)} %pad_add_fusion.pos.refs_0_, f32[512,128]{1,0:T(8,128)S(1)} %bitcast.33, f32[8,8,8,128]{3,2,1,0:T(8,128)S(1)} %get-tuple-element.223.refs_1_.z, ...), custom_call_target="tpu_custom_call" | custom-call | flops 2000000 | bytes 1048576 | tf_op jit(solution)/shard_map/last/pallas_call | solution.py:863
  194.4 4.2 %all-to-all-start.5 = ((f32[128,16,128]{2,1,0:T(8,128)}), f32[128,16,128]{2,1,0:T(8,128)S(1)}, u32[]{:S(2)}, u32[]{:S(2)}) async-start(f32[128,16,128]{2,1,0:T(8,128)} %bitcast.18), calls=%async_computation.5 | async-start | bytes 2097152 | tf_op jit(solution)/shard_map/all_to_all | solution.py:894
  200.7 16.7 %all-to-all-done.5 = f32[128,16,128]{2,1,0:T(8,128)S(1)} async-done(((f32[128,16,128]{2,1,0:T(8,128)}), f32[128,16,128]{2,1,0:T(8,128)S(1)}, u32[]{:S(2)}, u32[]{:S(2)}) %all-to-all-start.5) | async-done | bytes 1048608 | tf_op jit(solution)/shard_map/all_to_all | solution.py:894
  (97 shorter events, 57.9 us)
Async XLA Ops:
  5.1 3.3 %collective-permute-start.1 = (f32[8,8,128]{2,1,0:T(8,128)S(1)}, f32[8,8,128]{2,1,0:T(8,128)S(1)}, u32[]{:S(2)}, u32[]{:S(2)}) collective-permute-start(f32[8,8,128]{2,1,0:T(8,128)S(1)} %get-tuple-element.123), channel_id=1, source_target_pairs={{0,112},{16,32},{32,16},{48,64},{64,48},{80,96},{96,80},{112,0},{1... | collective-permute-start | bytes 98312 | tf_op jit(solution)/shard_map/ppermute | solution.py:885
  9.0 5.6 %collective-permute-start.2 = (f32[8,8,128]{2,1,0:T(8,128)S(1)}, f32[8,8,128]{2,1,0:T(8,128)S(1)}, u32[]{:S(2)}, u32[]{:S(2)}) collective-permute-start(f32[8,8,128]{2,1,0:T(8,128)S(1)} %get-tuple-element.125), channel_id=1, source_target_pairs={{0,1},{1,0},{2,3},{3,2},{4,5},{5,4},{6,7},{7,6},{8,9},{9,8},{10,11... | collective-permute-start | bytes 98312 | tf_op jit(solution)/shard_map/ppermute | solution.py:890
  10.4 6.1 %collective-permute-start.3 = (f32[8,8,128]{2,1,0:T(8,128)S(1)}, f32[8,8,128]{2,1,0:T(8,128)S(1)}, u32[]{:S(2)}, u32[]{:S(2)}) collective-permute-start(f32[8,8,128]{2,1,0:T(8,128)S(1)} %get-tuple-element.126), channel_id=1, source_target_pairs={{0,15},{1,2},{2,1},{3,4},{4,3},{5,6},{6,5},{7,8},{8,7},{9,10},{10,... | collective-permute-start | bytes 98312 | tf_op jit(solution)/shard_map/ppermute | solution.py:890
  40.9 3.3 %collective-permute-start.5 = (f32[8,8,128]{2,1,0:T(8,128)S(1)}, f32[8,8,128]{2,1,0:T(8,128)S(1)}, u32[]{:S(2)}, u32[]{:S(2)}) collective-permute-start(f32[8,8,128]{2,1,0:T(8,128)S(1)} %get-tuple-element.133), channel_id=1, source_target_pairs={{0,112},{16,32},{32,16},{48,64},{64,48},{80,96},{96,80},{112,0},{1... | collective-permute-start | bytes 98312 | tf_op jit(solution)/shard_map/ppermute | solution.py:885
  41.8 6.1 %collective-permute-start.7 = (f32[8,8,128]{2,1,0:T(8,128)S(1)}, f32[8,8,128]{2,1,0:T(8,128)S(1)}, u32[]{:S(2)}, u32[]{:S(2)}) collective-permute-start(f32[8,8,128]{2,1,0:T(8,128)S(1)} %get-tuple-element.135), channel_id=1, source_target_pairs={{0,15},{1,2},{2,1},{3,4},{4,3},{5,6},{6,5},{7,8},{8,7},{9,10},{10,... | collective-permute-start | bytes 98312 | tf_op jit(solution)/shard_map/ppermute | solution.py:890
  49.0 9.2 %collective-permute-start.10 = (f32[8,8,128]{2,1,0:T(8,128)S(1)}, f32[8,8,128]{2,1,0:T(8,128)S(1)}, u32[]{:S(2)}, u32[]{:S(2)}) collective-permute-start(f32[8,8,128]{2,1,0:T(8,128)S(1)} %get-tuple-element.141), channel_id=1, source_target_pairs={{0,1},{1,0},{2,3},{3,2},{4,5},{5,4},{6,7},{7,6},{8,9},{9,8},{10,11... | collective-permute-start | bytes 98312 | tf_op jit(solution)/shard_map/ppermute | solution.py:890
  49.1 9.1 %collective-permute-start.11 = (f32[8,8,128]{2,1,0:T(8,128)S(1)}, f32[8,8,128]{2,1,0:T(8,128)S(1)}, u32[]{:S(2)}, u32[]{:S(2)}) collective-permute-start(f32[8,8,128]{2,1,0:T(8,128)S(1)} %get-tuple-element.142), channel_id=1, source_target_pairs={{0,15},{1,2},{2,1},{3,4},{4,3},{5,6},{6,5},{7,8},{8,7},{9,10},{10,... | collective-permute-start | bytes 98312 | tf_op jit(solution)/shard_map/ppermute | solution.py:890
  50.1 8.1 %collective-permute-start.8 = (f32[8,8,128]{2,1,0:T(8,128)S(1)}, f32[8,8,128]{2,1,0:T(8,128)S(1)}, u32[]{:S(2)}, u32[]{:S(2)}) collective-permute-start(f32[8,8,128]{2,1,0:T(8,128)S(1)} %get-tuple-element.139), channel_id=1, source_target_pairs={{0,16},{16,0},{32,48},{48,32},{64,80},{80,64},{96,112},{112,96},{1... | collective-permute-start | bytes 98312 | tf_op jit(solution)/shard_map/ppermute | solution.py:885
  52.3 5.9 %collective-permute-start.9 = (f32[8,8,128]{2,1,0:T(8,128)S(1)}, f32[8,8,128]{2,1,0:T(8,128)S(1)}, u32[]{:S(2)}, u32[]{:S(2)}) collective-permute-start(f32[8,8,128]{2,1,0:T(8,128)S(1)} %get-tuple-element.140), channel_id=1, source_target_pairs={{0,112},{16,32},{32,16},{48,64},{64,48},{80,96},{96,80},{112,0},{1... | collective-permute-start | bytes 98312 | tf_op jit(solution)/shard_map/ppermute | solution.py:885
  80.4 3.3 %collective-permute-start.13 = (f32[8,8,128]{2,1,0:T(8,128)S(1)}, f32[8,8,128]{2,1,0:T(8,128)S(1)}, u32[]{:S(2)}, u32[]{:S(2)}) collective-permute-start(f32[8,8,128]{2,1,0:T(8,128)S(1)} %get-tuple-element.155), channel_id=1, source_target_pairs={{0,112},{16,32},{32,16},{48,64},{64,48},{80,96},{96,80},{112,0},{1... | collective-permute-start | bytes 98312 | tf_op jit(solution)/shard_map/ppermute | solution.py:885
  81.3 6.1 %collective-permute-start.15 = (f32[8,8,128]{2,1,0:T(8,128)S(1)}, f32[8,8,128]{2,1,0:T(8,128)S(1)}, u32[]{:S(2)}, u32[]{:S(2)}) collective-permute-start(f32[8,8,128]{2,1,0:T(8,128)S(1)} %get-tuple-element.157), channel_id=1, source_target_pairs={{0,15},{1,2},{2,1},{3,4},{4,3},{5,6},{6,5},{7,8},{8,7},{9,10},{10,... | collective-permute-start | bytes 98312 | tf_op jit(solution)/shard_map/ppermute | solution.py:890
  88.5 4.8 %collective-permute-start.16 = (f32[8,8,128]{2,1,0:T(8,128)S(1)}, f32[8,8,128]{2,1,0:T(8,128)S(1)}, u32[]{:S(2)}, u32[]{:S(2)}) collective-permute-start(f32[8,8,128]{2,1,0:T(8,128)S(1)} %get-tuple-element.164), channel_id=1, source_target_pairs={{0,16},{16,0},{32,48},{48,32},{64,80},{80,64},{96,112},{112,96},{1... | collective-permute-start | bytes 98312 | tf_op jit(solution)/shard_map/ppermute | solution.py:885
  90.5 3.3 %collective-permute-start.17 = (f32[8,8,128]{2,1,0:T(8,128)S(1)}, f32[8,8,128]{2,1,0:T(8,128)S(1)}, u32[]{:S(2)}, u32[]{:S(2)}) collective-permute-start(f32[8,8,128]{2,1,0:T(8,128)S(1)} %get-tuple-element.165), channel_id=1, source_target_pairs={{0,112},{16,32},{32,16},{48,64},{64,48},{80,96},{96,80},{112,0},{1... | collective-permute-start | bytes 98312 | tf_op jit(solution)/shard_map/ppermute | solution.py:885
  91.3 6.4 %collective-permute-start.19 = (f32[8,8,128]{2,1,0:T(8,128)S(1)}, f32[8,8,128]{2,1,0:T(8,128)S(1)}, u32[]{:S(2)}, u32[]{:S(2)}) collective-permute-start(f32[8,8,128]{2,1,0:T(8,128)S(1)} %get-tuple-element.167), channel_id=1, source_target_pairs={{0,15},{1,2},{2,1},{3,4},{4,3},{5,6},{6,5},{7,8},{8,7},{9,10},{10,... | collective-permute-start | bytes 98312 | tf_op jit(solution)/shard_map/ppermute | solution.py:890
  118.2 3.3 %collective-permute-start.21 = (f32[8,8,128]{2,1,0:T(8,128)S(1)}, f32[8,8,128]{2,1,0:T(8,128)S(1)}, u32[]{:S(2)}, u32[]{:S(2)}) collective-permute-start(f32[8,8,128]{2,1,0:T(8,128)S(1)} %get-tuple-element.179), channel_id=1, source_target_pairs={{0,112},{16,32},{32,16},{48,64},{64,48},{80,96},{96,80},{112,0},{1... | collective-permute-start | bytes 98312 | tf_op jit(solution)/shard_map/ppermute | solution.py:885
  119.0 6.1 %collective-permute-start.23 = (f32[8,8,128]{2,1,0:T(8,128)S(1)}, f32[8,8,128]{2,1,0:T(8,128)S(1)}, u32[]{:S(2)}, u32[]{:S(2)}) collective-permute-start(f32[8,8,128]{2,1,0:T(8,128)S(1)} %get-tuple-element.181), channel_id=1, source_target_pairs={{0,15},{1,2},{2,1},{3,4},{4,3},{5,6},{6,5},{7,8},{8,7},{9,10},{10,... | collective-permute-start | bytes 98312 | tf_op jit(solution)/shard_map/ppermute | solution.py:890
  126.3 4.8 %collective-permute-start.24 = (f32[8,8,128]{2,1,0:T(8,128)S(1)}, f32[8,8,128]{2,1,0:T(8,128)S(1)}, u32[]{:S(2)}, u32[]{:S(2)}) collective-permute-start(f32[8,8,128]{2,1,0:T(8,128)S(1)} %get-tuple-element.191), channel_id=1, source_target_pairs={{0,16},{16,0},{32,48},{48,32},{64,80},{80,64},{96,112},{112,96},{1... | collective-permute-start | bytes 98312 | tf_op jit(solution)/shard_map/ppermute | solution.py:885
  128.3 3.3 %collective-permute-start.25 = (f32[8,8,128]{2,1,0:T(8,128)S(1)}, f32[8,8,128]{2,1,0:T(8,128)S(1)}, u32[]{:S(2)}, u32[]{:S(2)}) collective-permute-start(f32[8,8,128]{2,1,0:T(8,128)S(1)} %get-tuple-element.192), channel_id=1, source_target_pairs={{0,112},{16,32},{32,16},{48,64},{64,48},{80,96},{96,80},{112,0},{1... | collective-permute-start | bytes 98312 | tf_op jit(solution)/shard_map/ppermute | solution.py:885
  129.1 6.4 %collective-permute-start.27 = (f32[8,8,128]{2,1,0:T(8,128)S(1)}, f32[8,8,128]{2,1,0:T(8,128)S(1)}, u32[]{:S(2)}, u32[]{:S(2)}) collective-permute-start(f32[8,8,128]{2,1,0:T(8,128)S(1)} %get-tuple-element.194), channel_id=1, source_target_pairs={{0,15},{1,2},{2,1},{3,4},{4,3},{5,6},{6,5},{7,8},{8,7},{9,10},{10,... | collective-permute-start | bytes 98312 | tf_op jit(solution)/shard_map/ppermute | solution.py:890
  155.9 3.3 %collective-permute-start.29 = (f32[8,8,128]{2,1,0:T(8,128)S(1)}, f32[8,8,128]{2,1,0:T(8,128)S(1)}, u32[]{:S(2)}, u32[]{:S(2)}) collective-permute-start(f32[8,8,128]{2,1,0:T(8,128)S(1)} %get-tuple-element.206), channel_id=1, source_target_pairs={{0,112},{16,32},{32,16},{48,64},{64,48},{80,96},{96,80},{112,0},{1... | collective-permute-start | bytes 98312 | tf_op jit(solution)/shard_map/ppermute | solution.py:885
  157.0 6.1 %collective-permute-start.31 = (f32[8,8,128]{2,1,0:T(8,128)S(1)}, f32[8,8,128]{2,1,0:T(8,128)S(1)}, u32[]{:S(2)}, u32[]{:S(2)}) collective-permute-start(f32[8,8,128]{2,1,0:T(8,128)S(1)} %get-tuple-element.208), channel_id=1, source_target_pairs={{0,15},{1,2},{2,1},{3,4},{4,3},{5,6},{6,5},{7,8},{8,7},{9,10},{10,... | collective-permute-start | bytes 98312 | tf_op jit(solution)/shard_map/ppermute | solution.py:890
  164.2 4.6 %collective-permute-start.32 = (f32[8,8,128]{2,1,0:T(8,128)S(1)}, f32[8,8,128]{2,1,0:T(8,128)S(1)}, u32[]{:S(2)}, u32[]{:S(2)}) collective-permute-start(f32[8,8,128]{2,1,0:T(8,128)S(1)} %get-tuple-element.218), channel_id=1, source_target_pairs={{0,16},{16,0},{32,48},{48,32},{64,80},{80,64},{96,112},{112,96},{1... | collective-permute-start | bytes 98312 | tf_op jit(solution)/shard_map/ppermute | solution.py:885
  166.8 6.1 %collective-permute-start.35 = (f32[8,8,128]{2,1,0:T(8,128)S(1)}, f32[8,8,128]{2,1,0:T(8,128)S(1)}, u32[]{:S(2)}, u32[]{:S(2)}) collective-permute-start(f32[8,8,128]{2,1,0:T(8,128)S(1)} %get-tuple-element.221), channel_id=1, source_target_pairs={{0,15},{1,2},{2,1},{3,4},{4,3},{5,6},{6,5},{7,8},{8,7},{9,10},{10,... | collective-permute-start | bytes 98312 | tf_op jit(solution)/shard_map/ppermute | solution.py:890
  194.4 23.0 %all-to-all-start.5 = ((f32[128,16,128]{2,1,0:T(8,128)}), f32[128,16,128]{2,1,0:T(8,128)S(1)}, u32[]{:S(2)}, u32[]{:S(2)}) async-start(f32[128,16,128]{2,1,0:T(8,128)} %bitcast.18), calls=%async_computation.5 | async-start | bytes 2097152 | tf_op jit(solution)/shard_map/all_to_all | solution.py:894
  (20 other events, 43.1 us)
where the time goes:
time: 219 us
  blocking collectives  88 us (40%)
  waiting for transfers between devices  53.1 us (24%)
  starting transfers between devices  39.3 us (18%)
  Pallas kernels  32.3 us (15%)
  local copies, waits for them, and re-layouts  4.98 us (2%)
    all_to_all x5, blocking collectives, everywhere(): lax.all_to_all(rows, ('row', 'height'), split_axis=0, concat_axis=0, tile...  88 us
    pallas_call x27, Pallas kernels, call(): pl.pallas_call(body, out_shape=[jax.ShapeDtypeStruct(*shape(o)) for o in...  32.3 us
    ppermute x9, waiting for transfers between devices, swap_z(): lax.ppermute(pair[1], 'height', b)  25.9 us
    ppermute x18, starting transfers between devices, swap_x(): return [lax.ppermute(pair[0], 'row', a), lax.ppermute(pair[1], 'row', b)]  20 us
    all_to_all x1, waiting for transfers between devices, everywhere(): lax.all_to_all(rows, ('row', 'height'), split_axis=0, concat_axis=0, tile...  16.7 us
    ppermute x9, starting transfers between devices, swap_z(): lax.ppermute(pair[1], 'height', b)  12.3 us
    ppermute x18, waiting for transfers between devices, swap_x(): return [lax.ppermute(pair[0], 'row', a), lax.ppermute(pair[1], 'row', b)]  8.52 us
    unnamed x14, local copies, waits for them, and re-layouts  4.98 us
  transfers between devices with their start and end apart: 37, of which 21 were waited for; matrix products, arithmetic and copies ran while one was open for 0% of the time, Pallas kernels for 3%

commit v1 on v0

--- a/solution.py
+++ b/solution.py
@@ -230,28 +230,36 @@
     return before, after
 
 
+MID, FACE_MU = 2.0 - 2.0 * W[0], 2.0 * W[0]
+SYM_F = (MID / (2.0 * FACE_MU)) ** 0.5
+SYM_M = -((FACE_MU / (2.0 * MID)) ** 0.5)
+A0, B0 = (MID + FACE_MU / 2.0) / 2.0**0.5, FACE_MU / (4.0 * 2.0**0.5)
+A1, B1 = -SYM_F * FACE_MU / 2.0, SYM_F * FACE_MU / 4.0
+C2 = FACE_MU**0.5 / 4.0
+LAM = (
+    0.0,
+    float(2.0 * (K_[0, 0] + K_[0, 7])) * (SYM_F - SYM_M) ** 2,
+    float(2.0 * (K_[0, 0] - K_[0, 7])) / FACE_MU,
+)
+
+
 def spread3(v, before, after):
-    return (v, 0.5 * v + 0.25 * (before + after), 0.25 * (before - after))
+    both = before + after
+    return (A0 * v + B0 * both, A1 * v + B1 * both, C2 * (before - after))
+
+
+def back3(duals):
+    t, u = B0 * duals[0] + B1 * duals[1], C2 * duals[2]
+    return A0 * duals[0] + A1 * duals[1], t + u, t - u
 
 
 def gather3(duals, axis):
-    m, f, a = duals
-    g, h = 0.25 * (f + a), 0.25 * (f - a)
-    n = m.shape[axis]
-    p = lax.broadcasted_iota(jnp.int32, m.shape, axis)
+    own, g, h = back3(duals)
+    n = own.shape[axis]
+    p = lax.broadcasted_iota(jnp.int32, own.shape, axis)
     up = jnp.where(p == n - 1, h, pltpu.roll(g, n - 1, axis))
     down = jnp.where(p == 0, g, pltpu.roll(h, 1, axis))
-    return m + 0.5 * f + up + down
-
-
-MU = (2.0 - 2.0 * W[0], 2.0 * W[0], 2.0 * W[0])
-KS = float(2.0 * (K_[0, 0] + K_[0, 7]))
-KA = float(2.0 * (K_[0, 0] - K_[0, 7]))
-
-
-def stiff3(q):
-    d = q[1] - q[0]
-    return ((-KS / MU[0]) * d, (KS / MU[1]) * d, (KA / MU[2]) * q[2])
+    return own + (up + down)
 
 
 def coarse_operator(d, kc_ref, cc_ref, tmp_ref):
@@ -261,54 +269,38 @@
             xs = spread3(ys[c], *shift_pair(ys[c], 0))
             for a in range(3):
                 tmp_ref[(a * 3 + c) * NZ + h] = xs[a]
-    part = []
+    keys = [(a, c) for a in range(3) for c in range(3)]
+    res, kept, after = [], {}, {}
+
+    def finish(vals):
+        return gather3([gather3([vals[a, c] for a in range(3)], 0) for c in range(3)], 1)
+
     for h in range(NZ):
         lo, hi = max(h - 1, 0), min(h + 1, NZ - 1)
-        q = {}
-        for a in range(3):
-            for c in range(3):
-                base = (a * 3 + c) * NZ
-                zs = spread3(tmp_ref[base + h], tmp_ref[base + lo], tmp_ref[base + hi])
-                for b in range(3):
-                    q[a, b, c] = zs[b]
-        acc = {key: None for key in q}
-
-        def add(key, val):
-            acc[key] = val if acc[key] is None else acc[key] + val
-
-        for b in range(3):
-            for c in range(3):
-                for n, val in enumerate(stiff3([q[a, b, c] for a in range(3)])):
-                    add((n, b, c), val)
-        for a in range(3):
-            for c in range(3):
-                for n, val in enumerate(stiff3([q[a, b, c] for b in range(3)])):
-                    add((a, n, c), val)
-        for a in range(3):
+        kh, ch = kc_ref[h], cc_ref[h]
+        factor, final = {}, {}
+        for a, c in keys:
+            base = (a * 3 + c) * NZ
+            zs = spread3(tmp_ref[base + h], tmp_ref[base + lo], tmp_ref[base + hi])
+            duals = []
             for b in range(3):
-                for n, val in enumerate(stiff3([q[a, b, c] for c in range(3)])):
-                    add((a, b, n), val)
-        kh, ch = kc_ref[h], cc_ref[h]
-        outs = []
-        for b in range(3):
-            cols = []
-            for c in range(3):
-                duals = [
-                    (MU[a] * MU[b] * MU[c]) * (kh * acc[a, b, c] + ch * q[a, b, c])
-                    for a in range(3)
-                ]
-                cols.append(gather3(duals, 0))
-            outs.append(gather3(cols, 1))
-        part.append(outs)
-    res = []
-    for h in range(NZ):
-        m, f, _ = part[h]
-        v = m + 0.5 * f
-        g = lambda n: 0.25 * (part[n][1] + part[n][2])
-        l = lambda n: 0.25 * (part[n][1] - part[n][2])
-        v = v + (g(h + 1) if h < NZ - 1 else l(h))
-        v = v + (l(h - 1) if h > 0 else g(h))
-        res.append(v)
+                kind = tuple(sorted((a, b, c)))
+                if kind not in factor:
+                    lam = sum(LAM[n] for n in kind)
+                    factor[kind] = kh * lam + ch if lam else ch
+                duals.append(factor[kind] * zs[b])
+            own, g, hh = back3(duals)
+            if h > 0:
+                final[a, c] = kept[a, c] + g
+                own = own + after[a, c]
+            else:
+                own = own + g
+            if h == NZ - 1:
+                own = own + hh
+            kept[a, c], after[a, c] = own, hh
+        if h > 0:
+            res.append(finish(final))
+    res.append(finish(kept))
     return res
 
 
@@ -427,19 +419,11 @@
     return [got_ref[pl.ds(4 * h + which, NX, stride=4 * NZ), :] for h in range(NZ)]
 
 
-def heat_kernel(pos, heat, cond, marks, f, ma, mb, kc, mk, buf, sems):
-    copies = [
-        pltpu.make_async_copy(src, dst, sems.at[n])
-        for n, (src, dst) in enumerate(((heat, buf), (cond, kc), (marks, mk)))
-    ]
-    for copy in copies:
-        copy.start()
+def heat_kernel(pos, heat, f, ma, mb):
     _, _, _, _, even = place(pos)
     wk = kvec(W)
-    for copy in copies:
-        copy.wait()
     for i in range(8):
-        new = [(W[i] * W[j]) * wk * buf[i, j] for j in range(8)]
+        new = [(W[i] * W[j]) * wk * heat[i, j] for j in range(8)]
         for j in range(8):
             f[i, j] = new[j]
     put_pair(even[0], f[0], f[E], (ma, mb))
@@ -452,15 +436,15 @@
     put_pair(even[1], out[:, 0], out[:, E], (ma, mb))
 
 
-def first_rows_kernel(pos, f, ra, rb, kc, marks, out, rows):
+def first_rows_kernel(pos, f, ra, rb, both, out, rows):
     _, _, has, frac, even = place(pos)
     out[...] = f[...]
     add_faces_z(out, (ra, rb), has, even)
     assemble_aisle(out)
     tile = field_sum(lambda i, j: out[i, j], frac) * own_mult()
     restricted = jnp.sum(tile, axis=0, keepdims=True)
-    cap = jnp.where(marks[...] == 1, jnp.float32(HEAT_SOLID), jnp.float32(HEAT_AIR))
-    block = jnp.concatenate([kc[...], cap, restricted, jnp.zeros((1, NY), F32)], axis=0)
+    cap = jnp.where(both[1:2] == 1.0, jnp.float32(HEAT_SOLID), jnp.float32(HEAT_AIR))
+    block = jnp.concatenate([both[0:1], cap, restricted, jnp.zeros((1, NY), F32)], axis=0)
     rows[...] = jnp.broadcast_to(block[None], rows.shape)
 
 
@@ -746,15 +730,10 @@
 SLOTS = 16
 
 
-def slots_kernel(own_in, elem_in, side_in, target_in, table, owners, own, elem, side, target, sems):
-    pairs = ((own_in, own), (elem_in, elem), (side_in, side), (target_in, target))
-    copies = [pltpu.make_async_copy(src, dst, sems.at[n]) for n, (src, dst) in enumerate(pairs)]
-    for copy in copies:
-        copy.start()
-    for copy in copies:
-        copy.wait()
+def slots_kernel(ints, table, owners):
+    own, elem, side, target = (ints[n : n + 1] for n in range(4))
     faces = own.shape[1]
-    row = own[...].astype(F32)
+    row = own.astype(F32)
     col = jnp.broadcast_to(row, (NY, faces)).T
     ranks = []
     for s in range(0, faces, NY):
@@ -765,7 +744,7 @@
     rank = jnp.concatenate(ranks, axis=1)
     slot = row * SLOTS + rank
     vals = jnp.concatenate(
-        [elem[...].astype(F32) + 1.0, side[...].astype(F32), jnp.zeros((6, faces), F32)], axis=0
+        [elem.astype(F32) + 1.0, side.astype(F32), jnp.zeros((6, faces), F32)], axis=0
     ).astype(jnp.bfloat16)
     step = 256
     for s in range(0, table.shape[0], step):
@@ -779,7 +758,7 @@
     dev = lax.broadcasted_iota(jnp.int32, (devices, faces), 0).astype(F32)
     hot = jnp.where(dev == row, 1.0, 0.0).astype(jnp.bfloat16)
     at = lax.broadcasted_iota(jnp.int32, (128, faces), 0).astype(F32)
-    marked = jnp.where(at == rank, target[...].astype(F32) + 1.0, 0.0).astype(jnp.bfloat16)
+    marked = jnp.where(at == rank, target.astype(F32) + 1.0, 0.0).astype(jnp.bfloat16)
     owners[...] = lax.dot_general(hot, marked, NT, preferred_element_type=F32) - 1.0
 
 
@@ -849,23 +828,17 @@
     out[...] = acc.T
 
 
-def call(body, name, outs, args, scratch=(), copied=()):
+def call(body, name, outs, args, scratch=()):
     vmem = pl.BlockSpec(memory_space=pltpu.VMEM)
+    smem = pl.BlockSpec(memory_space=pltpu.SMEM)
     shape = lambda o: o if isinstance(o[0], tuple) else (o, F32)
-
-    def spec(n, a):
-        if n in copied:
-            return pl.BlockSpec(memory_space=pltpu.HBM)
-        if a.dtype == jnp.int32 and a.shape == (2,):
-            return pl.BlockSpec(memory_space=pltpu.SMEM)
-        return vmem
-
+    scalars = lambda a: a.dtype == jnp.int32 and a.shape == (2,)
     return pl.pallas_call(
         body,
         out_shape=[jax.ShapeDtypeStruct(*shape(o)) for o in outs],
-        in_specs=[spec(n, a) for n, a in enumerate(args)],
+        in_specs=[smem if scalars(a) else vmem for a in args],
         out_specs=[vmem] * len(outs),
-        scratch_shapes=[pltpu.VMEM(*shape(s)) if isinstance(s, tuple) else s for s in scratch],
+        scratch_shapes=[pltpu.VMEM(s, F32) for s in scratch],
         compiler_params=pltpu.CompilerParams(vmem_limit_bytes=24 * 1024 * 1024),
         cost_estimate=pl.CostEstimate(
             flops=2_000_000, bytes_accessed=1 << 20, transcendentals=0
@@ -874,20 +847,32 @@
     )(*args)
 
 
-def pair_perms(n):
-    first = [(i, i ^ 1) for i in range(n)]
-    second = [(i, (i + 1) % n if i % 2 else (i - 1) % n) for i in range(n)]
-    return first, second
+def pairs(axis, second):
+    out = []
+    for x in range(NX):
+        for z in range(NZ):
+            here = [x, z]
+            n, last = here[axis], (NX, NZ)[axis] - 1
+            if not second:
+                here[axis] = n ^ 1
+            elif n in (0, last):
+                here[1 - axis] ^= 1
+            else:
+                here[axis] = n + 1 if n % 2 else n - 1
+            out.append((x * NZ + z, here[0] * NZ + here[1]))
+    return out
+
+
+def swap(pair, axis):
+    return [lax.ppermute(v, ("row", "height"), pairs(axis, n == 1)) for n, v in enumerate(pair)]
 
 
 def swap_x(pair):
-    a, b = pair_perms(NX)
-    return [lax.ppermute(pair[0], "row", a), lax.ppermute(pair[1], "row", b)]
+    return swap(pair, 0)
 
 
 def swap_z(pair):
-    a, b = pair_perms(NZ)
-    return [lax.ppermute(pair[0], "height", a), lax.ppermute(pair[1], "height", b)]
+    return swap(pair, 1)
 
 
 def everywhere(rows):
@@ -897,25 +882,15 @@
 def shards(heat, conductivity, marks, face_owner, face_element, face_side, owner_element):
     devices = NX * NZ
     pos = jnp.stack([lax.axis_index("row"), lax.axis_index("height")]).astype(jnp.int32)
-    row = lambda a: a.reshape(1, -1)
-    line = ((1, NY), F32)
-    faces = ((1, face_element.shape[0]), jnp.int32)
-    f, ma, mb, cond, marks = call(
-        heat_kernel,
-        "heat",
-        [FIELD, FACE, FACE, line, ((1, NY), jnp.int32)],
-        [pos, heat.reshape(FIELD), row(conductivity), row(marks)],
-        scratch=[FIELD, pltpu.SemaphoreType.DMA((3,))],
-        copied=(1, 2, 3),
-    )
+    f, ma, mb = call(heat_kernel, "heat", [FIELD, FACE, FACE], [pos, heat.reshape(FIELD)])
     ra, rb = swap_x((ma, mb))
+    both = jnp.stack([conductivity.reshape(-1), marks.reshape(-1).astype(F32)])
+    ints = jnp.stack([face_owner.reshape(-1), face_element, face_side, owner_element])
     table, owners = call(
         slots_kernel,
         "slots",
         [((devices * SLOTS, 6 * NY), jnp.bfloat16), (devices, 128)],
-        [row(face_owner), row(face_element), row(face_side), row(owner_element)],
-        scratch=[faces] * 4 + [pltpu.SemaphoreType.DMA((4,))],
-        copied=(0, 1, 2, 3),
+        [ints],
     )
     f, ma, mb = call(heat_z_kernel, "heat_z", [FIELD, FACE, FACE], [pos, f, ra, rb])
     ra, rb = swap_z((ma, mb))
@@ -923,7 +898,7 @@
         first_rows_kernel,
         "first_rows",
         [FIELD, (devices, 4, NY)],
-        [pos, f, ra, rb, cond, marks],
+        [pos, f, ra, rb, both],
     )
     got0 = everywhere(rows).reshape(devices * 4, NY)
     kc, cc, cf, rc, nb, dinv, z, f, *msgs = call(

time: 219 us -> 205 us (0.936)
  waiting for transfers between devices: 53.1 us -> 26 us
  blocking collectives: 88 us -> 107 us
  local copies, waits for them, and re-layouts: 4.98 us -> 0.95 us
  starting transfers between devices: 39.3 us -> 36.3 us
    ppermute x36, waiting for transfers between devices: 36.3 us -> 9.23 us  [swap(): lax.ppermute(v, ('row', 'height'), pairs(axis, n == 1))]
    all_to_all x5, blocking collectives: 88 us -> 107 us  [everywhere(): lax.all_to_all(rows, ('row', 'height'), split_axis=0, concat_axis=0, tile...]
    unnamed x14 -> x2, local copies, waits for them, and re-layouts: 4.98 us -> 0.95 us
    ppermute x36, starting transfers between devices: 35.1 us -> 32.1 us  [swap(): lax.ppermute(v, ('row', 'height'), pairs(axis, n == 1))]
  transfers between devices with their start and end apart: 37 -> 37, of which waited for: 21 -> 15; matrix products, arithmetic and copies ran while one was open for 0% -> 1% of each run, Pallas kernels for 3% -> 4%
where the time goes in v1:
time: 205 us; the launch traced here: 204 us
  blocking collectives  107 us (52%)
  starting transfers between devices  36.3 us (18%)
  Pallas kernels  31.3 us (15%)
  waiting for transfers between devices  26 us (13%)
  other arithmetic  2.14 us (1%)
    all_to_all x5, blocking collectives, everywhere(): lax.all_to_all(rows, ('row', 'height'), split_axis=0, concat_axis=0, tile...  107 us
    ppermute x36, starting transfers between devices, swap(): lax.ppermute(v, ('row', 'height'), pairs(axis, n == 1))  32.1 us
    pallas_call x27, Pallas kernels, call(): pl.pallas_call(body, out_shape=[jax.ShapeDtypeStruct(*shape(o)) for o in...  31.3 us
    all_to_all x1, waiting for transfers between devices, everywhere(): lax.all_to_all(rows, ('row', 'height'), split_axis=0, concat_axis=0, tile...  16.7 us
    ppermute x36, waiting for transfers between devices, swap(): lax.ppermute(v, ('row', 'height'), pairs(axis, n == 1))  9.23 us
    all_to_all x1, starting transfers between devices, everywhere(): lax.all_to_all(rows, ('row', 'height'), split_axis=0, concat_axis=0, tile...  4.2 us
  transfers between devices with their start and end apart: 37, of which 15 were waited for; matrix products, arithmetic and copies ran while one was open for 1% of the time, Pallas kernels for 4%

profile of v1, /device:TPU:1, one launch (start us, length us, event | category | flops | bytes accessed | tf_op | source)
XLA Modules:
  0.0 204.4 jit_solution(9623015270855410311)
XLA Ops:
  2.2 1.5 collective-permute-start
  3.7 1.7 collective-permute-start.1
  7.9 1.4 collective-permute-start.2
  11.6 24.7 %all_to_all.30 = f32[128,4,128]{2,1,0:T(4,128)S(1)} all-to-all(f32[128,4,128]{2,1,0:T(4,128)S(1)} %get-tuple-element.125), channel_id=1, replica_groups=mesh['row'=8,'height'=16] {'row','height'}, dimensions={0} | all-to-all | bytes 524288 | tf_op jit(solution)/shard_map/all_to_all | solution.py:879
  36.3 1.4 setup.1
  40.7 1.5 collective-permute-done.5.r1
  44.8 1.6 collective-permute-start.11
  46.4 1.6 collective-permute-start.9
  48.7 1.5 slots.1
  51.7 18.6 %all_to_all.31 = f32[128,4,128]{2,1,0:T(4,128)S(1)} all-to-all(f32[128,4,128]{2,1,0:T(4,128)S(1)} %get-tuple-element.143), channel_id=1, replica_groups=mesh['row'=8,'height'=16] {'row','height'}, dimensions={0} | all-to-all | bytes 524288 | tf_op jit(solution)/shard_map/all_to_all | solution.py:879
  70.2 2.5 %step.3 = (f32[8,8,8,128]{3,2,1,0:T(8,128)S(1)}, f32[16,8,128]{2,1,0:T(8,128)S(1)}, f32[8,8,8,128]{3,2,1,0:T(8,128)S(1)}, f32[8,8,8,128]{3,2,1,0:T(8,128)S(1)}, ...) custom-call(s32[2]{0:T(128)S(1)} %pad_add_fusion.1.pos.refs_0_, ...), custom_call_target="tpu_custom_call" | custom-call | flops 2000000 | bytes 1048576 | tf_op jit(solution)/shard_map/step/pallas_call | solution.py:836
  75.8 1.3 collective-permute-done.13.r1
  80.7 1.7 collective-permute-start.18
  84.5 21.2 %all_to_all.32 = f32[128,4,128]{2,1,0:T(4,128)S(1)} all-to-all(f32[128,4,128]{2,1,0:T(4,128)S(1)} %get-tuple-element.170), channel_id=1, replica_groups=mesh['row'=8,'height'=16] {'row','height'}, dimensions={0} | all-to-all | bytes 524288 | tf_op jit(solution)/shard_map/all_to_all | solution.py:879
  105.6 2.5 %step.4 = (f32[8,8,8,128]{3,2,1,0:T(8,128)S(1)}, f32[16,8,128]{2,1,0:T(8,128)S(1)}, f32[8,8,8,128]{3,2,1,0:T(8,128)S(1)}, f32[8,8,8,128]{3,2,1,0:T(8,128)S(1)}, ...) custom-call(s32[2]{0:T(128)S(1)} %pad_add_fusion.1.pos.refs_0_, ...), custom_call_target="tpu_custom_call" | custom-call | flops 2000000 | bytes 1048576 | tf_op jit(solution)/shard_map/step/pallas_call | solution.py:836
  115.9 1.7 collective-permute-start.26
  119.7 21.2 %all_to_all.33 = f32[128,4,128]{2,1,0:T(4,128)S(1)} all-to-all(f32[128,4,128]{2,1,0:T(4,128)S(1)} %get-tuple-element.197), channel_id=1, replica_groups=mesh['row'=8,'height'=16] {'row','height'}, dimensions={0} | all-to-all | bytes 524288 | tf_op jit(solution)/shard_map/all_to_all | solution.py:879
  140.9 2.5 %step.5 = (f32[8,8,8,128]{3,2,1,0:T(8,128)S(1)}, f32[16,8,128]{2,1,0:T(8,128)S(1)}, f32[8,8,8,128]{3,2,1,0:T(8,128)S(1)}, f32[8,8,8,128]{3,2,1,0:T(8,128)S(1)}, ...) custom-call(s32[2]{0:T(128)S(1)} %pad_add_fusion.1.pos.refs_0_, ...), custom_call_target="tpu_custom_call" | custom-call | flops 2000000 | bytes 1048576 | tf_op jit(solution)/shard_map/step/pallas_call | solution.py:836
  151.2 1.7 collective-permute-start.34
  155.0 21.2 %all_to_all.34 = f32[128,4,128]{2,1,0:T(4,128)S(1)} all-to-all(f32[128,4,128]{2,1,0:T(4,128)S(1)} %get-tuple-element.224), channel_id=1, replica_groups=mesh['row'=8,'height'=16] {'row','height'}, dimensions={0} | all-to-all | bytes 524288 | tf_op jit(solution)/shard_map/all_to_all | solution.py:879
  176.2 4.0 %last.1 = (f32[8,8,8,128]{3,2,1,0:T(8,128)}, f32[2048,128]{1,0:T(8,128)}, f32[4,8,128]{2,1,0:T(8,128)S(1)}, f32[16,8,128]{2,1,0:T(8,128)S(1)}) custom-call(s32[2]{0:T(128)S(1)} %pad_add_fusion.1.pos.refs_0_, f32[512,128]{1,0:T(8,128)S(1)} %bitcast.34, f32[8,8,8,128]{3,2,1,0:T(8,128)S(1)} %get-tuple-element.219.refs_1_.z, ...), custom_call_target="tpu_custom_call" | custom-call | flops 2000000 | bytes 1048576 | tf_op jit(solution)/shard_map/last/pallas_call | solution.py:836
  180.2 4.2 %all-to-all-start.5 = ((f32[128,16,128]{2,1,0:T(8,128)}), f32[128,16,128]{2,1,0:T(8,128)S(1)}, u32[]{:S(2)}, u32[]{:S(2)}) async-start(f32[128,16,128]{2,1,0:T(8,128)} %bitcast.18), calls=%async_computation.5 | async-start | bytes 2097152 | tf_op jit(solution)/shard_map/all_to_all | solution.py:879
  184.8 1.7 residual.1
  186.5 16.7 %all-to-all-done.5 = f32[128,16,128]{2,1,0:T(8,128)S(1)} async-done(((f32[128,16,128]{2,1,0:T(8,128)}), f32[128,16,128]{2,1,0:T(8,128)S(1)}, u32[]{:S(2)}, u32[]{:S(2)}) %all-to-all-start.5) | async-done | bytes 1048608 | tf_op jit(solution)/shard_map/all_to_all | solution.py:879
  (88 shorter events, 43.7 us)
Async XLA Ops:
  2.2 3.9 %collective-permute-start = (f32[8,8,128]{2,1,0:T(8,128)S(1)}, f32[8,8,128]{2,1,0:T(8,128)S(1)}, u32[]{:S(2)}, u32[]{:S(2)}) collective-permute-start(f32[8,8,128]{2,1,0:T(8,128)S(1)} %get-tuple-element.120), channel_id=1, source_target_pairs={{0,16},{1,17},{2,18},{3,19},{4,20},{5,21},{6,22},{7,23},{8,24},{9,... | collective-permute-start | bytes 98312 | tf_op jit(solution)/shard_map/ppermute | solution.py:867
  3.7 3.6 %collective-permute-start.1 = (f32[8,8,128]{2,1,0:T(8,128)S(1)}, f32[8,8,128]{2,1,0:T(8,128)S(1)}, u32[]{:S(2)}, u32[]{:S(2)}) collective-permute-start(f32[8,8,128]{2,1,0:T(8,128)S(1)} %get-tuple-element.121), channel_id=1, source_target_pairs={{0,1},{1,0},{2,3},{3,2},{4,5},{5,4},{6,7},{7,6},{8,9},{9,8},{10,11... | collective-permute-start | bytes 98312 | tf_op jit(solution)/shard_map/ppermute | solution.py:867
  38.5 3.6 %collective-permute-start.5 = (f32[8,8,128]{2,1,0:T(8,128)S(1)}, f32[8,8,128]{2,1,0:T(8,128)S(1)}, u32[]{:S(2)}, u32[]{:S(2)}) collective-permute-start(f32[8,8,128]{2,1,0:T(8,128)S(1)} %get-tuple-element.129), channel_id=1, source_target_pairs={{0,1},{1,0},{2,3},{3,2},{4,5},{5,4},{6,7},{7,6},{8,9},{9,8},{10,11... | collective-permute-start | bytes 98312 | tf_op jit(solution)/shard_map/ppermute | solution.py:867
  39.1 3.4 %collective-permute-start.6 = (f32[8,8,128]{2,1,0:T(8,128)S(1)}, f32[8,8,128]{2,1,0:T(8,128)S(1)}, u32[]{:S(2)}, u32[]{:S(2)}) collective-permute-start(f32[8,8,128]{2,1,0:T(8,128)S(1)} %get-tuple-element.130), channel_id=1, source_target_pairs={{0,1},{1,0},{2,3},{3,2},{4,5},{5,4},{6,7},{7,6},{8,9},{9,8},{10,11... | collective-permute-start | bytes 98312 | tf_op jit(solution)/shard_map/ppermute | solution.py:867
  43.6 7.3 %collective-permute-start.10 = (f32[8,8,128]{2,1,0:T(8,128)S(1)}, f32[8,8,128]{2,1,0:T(8,128)S(1)}, u32[]{:S(2)}, u32[]{:S(2)}) collective-permute-start(f32[8,8,128]{2,1,0:T(8,128)S(1)} %get-tuple-element.137), channel_id=1, source_target_pairs={{0,1},{1,0},{2,3},{3,2},{4,5},{5,4},{6,7},{7,6},{8,9},{9,8},{10,11... | collective-permute-start | bytes 98312 | tf_op jit(solution)/shard_map/ppermute | solution.py:867
  44.8 6.1 %collective-permute-start.11 = (f32[8,8,128]{2,1,0:T(8,128)S(1)}, f32[8,8,128]{2,1,0:T(8,128)S(1)}, u32[]{:S(2)}, u32[]{:S(2)}) collective-permute-start(f32[8,8,128]{2,1,0:T(8,128)S(1)} %get-tuple-element.138), channel_id=1, source_target_pairs={{0,16},{1,2},{2,1},{3,4},{4,3},{5,6},{6,5},{7,8},{8,7},{9,10},{10,... | collective-permute-start | bytes 98312 | tf_op jit(solution)/shard_map/ppermute | solution.py:867
  46.4 4.5 %collective-permute-start.8 = (f32[8,8,128]{2,1,0:T(8,128)S(1)}, f32[8,8,128]{2,1,0:T(8,128)S(1)}, u32[]{:S(2)}, u32[]{:S(2)}) collective-permute-start(f32[8,8,128]{2,1,0:T(8,128)S(1)} %get-tuple-element.135), channel_id=1, source_target_pairs={{0,16},{1,17},{2,18},{3,19},{4,20},{5,21},{6,22},{7,23},{8,24},{9,... | collective-permute-start | bytes 98312 | tf_op jit(solution)/shard_map/ppermute | solution.py:867
  46.4 4.5 %collective-permute-start.9 = (f32[8,8,128]{2,1,0:T(8,128)S(1)}, f32[8,8,128]{2,1,0:T(8,128)S(1)}, u32[]{:S(2)}, u32[]{:S(2)}) collective-permute-start(f32[8,8,128]{2,1,0:T(8,128)S(1)} %get-tuple-element.136), channel_id=1, source_target_pairs={{0,1},{1,0},{2,3},{3,2},{4,5},{5,4},{6,7},{7,6},{8,9},{9,8},{10,11... | collective-permute-start | bytes 98312 | tf_op jit(solution)/shard_map/ppermute | solution.py:867
  73.5 3.6 %collective-permute-start.13 = (f32[8,8,128]{2,1,0:T(8,128)S(1)}, f32[8,8,128]{2,1,0:T(8,128)S(1)}, u32[]{:S(2)}, u32[]{:S(2)}) collective-permute-start(f32[8,8,128]{2,1,0:T(8,128)S(1)} %get-tuple-element.151), channel_id=1, source_target_pairs={{0,1},{1,0},{2,3},{3,2},{4,5},{5,4},{6,7},{7,6},{8,9},{9,8},{10,11... | collective-permute-start | bytes 98312 | tf_op jit(solution)/shard_map/ppermute | solution.py:867
  74.1 3.4 %collective-permute-start.14 = (f32[8,8,128]{2,1,0:T(8,128)S(1)}, f32[8,8,128]{2,1,0:T(8,128)S(1)}, u32[]{:S(2)}, u32[]{:S(2)}) collective-permute-start(f32[8,8,128]{2,1,0:T(8,128)S(1)} %get-tuple-element.152), channel_id=1, source_target_pairs={{0,1},{1,0},{2,3},{3,2},{4,5},{5,4},{6,7},{7,6},{8,9},{9,8},{10,11... | collective-permute-start | bytes 98312 | tf_op jit(solution)/shard_map/ppermute | solution.py:867
  78.8 4.5 %collective-permute-start.16 = (f32[8,8,128]{2,1,0:T(8,128)S(1)}, f32[8,8,128]{2,1,0:T(8,128)S(1)}, u32[]{:S(2)}, u32[]{:S(2)}) collective-permute-start(f32[8,8,128]{2,1,0:T(8,128)S(1)} %get-tuple-element.160), channel_id=1, source_target_pairs={{0,16},{1,17},{2,18},{3,19},{4,20},{5,21},{6,22},{7,23},{8,24},{9,... | collective-permute-start | bytes 98312 | tf_op jit(solution)/shard_map/ppermute | solution.py:867
  79.6 3.6 %collective-permute-start.17 = (f32[8,8,128]{2,1,0:T(8,128)S(1)}, f32[8,8,128]{2,1,0:T(8,128)S(1)}, u32[]{:S(2)}, u32[]{:S(2)}) collective-permute-start(f32[8,8,128]{2,1,0:T(8,128)S(1)} %get-tuple-element.161), channel_id=1, source_target_pairs={{0,1},{1,0},{2,3},{3,2},{4,5},{5,4},{6,7},{7,6},{8,9},{9,8},{10,11... | collective-permute-start | bytes 98312 | tf_op jit(solution)/shard_map/ppermute | solution.py:867
  108.2 3.2 %collective-permute-start.20 = (f32[8,8,128]{2,1,0:T(8,128)S(1)}, f32[8,8,128]{2,1,0:T(8,128)S(1)}, u32[]{:S(2)}, u32[]{:S(2)}) collective-permute-start(f32[8,8,128]{2,1,0:T(8,128)S(1)} %get-tuple-element.174), channel_id=1, source_target_pairs={{0,16},{1,17},{2,18},{3,19},{4,20},{5,21},{6,22},{7,23},{8,24},{9,... | collective-permute-start | bytes 98312 | tf_op jit(solution)/shard_map/ppermute | solution.py:867
  109.0 3.6 %collective-permute-start.21 = (f32[8,8,128]{2,1,0:T(8,128)S(1)}, f32[8,8,128]{2,1,0:T(8,128)S(1)}, u32[]{:S(2)}, u32[]{:S(2)}) collective-permute-start(f32[8,8,128]{2,1,0:T(8,128)S(1)} %get-tuple-element.175), channel_id=1, source_target_pairs={{0,1},{1,0},{2,3},{3,2},{4,5},{5,4},{6,7},{7,6},{8,9},{9,8},{10,11... | collective-permute-start | bytes 98312 | tf_op jit(solution)/shard_map/ppermute | solution.py:867
  109.5 3.4 %collective-permute-start.22 = (f32[8,8,128]{2,1,0:T(8,128)S(1)}, f32[8,8,128]{2,1,0:T(8,128)S(1)}, u32[]{:S(2)}, u32[]{:S(2)}) collective-permute-start(f32[8,8,128]{2,1,0:T(8,128)S(1)} %get-tuple-element.176), channel_id=1, source_target_pairs={{0,1},{1,0},{2,3},{3,2},{4,5},{5,4},{6,7},{7,6},{8,9},{9,8},{10,11... | collective-permute-start | bytes 98312 | tf_op jit(solution)/shard_map/ppermute | solution.py:867
  109.8 3.1 %collective-permute-start.23 = (f32[8,8,128]{2,1,0:T(8,128)S(1)}, f32[8,8,128]{2,1,0:T(8,128)S(1)}, u32[]{:S(2)}, u32[]{:S(2)}) collective-permute-start(f32[8,8,128]{2,1,0:T(8,128)S(1)} %get-tuple-element.177), channel_id=1, source_target_pairs={{0,16},{1,2},{2,1},{3,4},{4,3},{5,6},{6,5},{7,8},{8,7},{9,10},{10,... | collective-permute-start | bytes 98312 | tf_op jit(solution)/shard_map/ppermute | solution.py:867
  114.0 4.5 %collective-permute-start.24 = (f32[8,8,128]{2,1,0:T(8,128)S(1)}, f32[8,8,128]{2,1,0:T(8,128)S(1)}, u32[]{:S(2)}, u32[]{:S(2)}) collective-permute-start(f32[8,8,128]{2,1,0:T(8,128)S(1)} %get-tuple-element.187), channel_id=1, source_target_pairs={{0,16},{1,17},{2,18},{3,19},{4,20},{5,21},{6,22},{7,23},{8,24},{9,... | collective-permute-start | bytes 98312 | tf_op jit(solution)/shard_map/ppermute | solution.py:867
  114.9 3.6 %collective-permute-start.25 = (f32[8,8,128]{2,1,0:T(8,128)S(1)}, f32[8,8,128]{2,1,0:T(8,128)S(1)}, u32[]{:S(2)}, u32[]{:S(2)}) collective-permute-start(f32[8,8,128]{2,1,0:T(8,128)S(1)} %get-tuple-element.188), channel_id=1, source_target_pairs={{0,1},{1,0},{2,3},{3,2},{4,5},{5,4},{6,7},{7,6},{8,9},{9,8},{10,11... | collective-permute-start | bytes 98312 | tf_op jit(solution)/shard_map/ppermute | solution.py:867
  143.5 3.2 %collective-permute-start.28 = (f32[8,8,128]{2,1,0:T(8,128)S(1)}, f32[8,8,128]{2,1,0:T(8,128)S(1)}, u32[]{:S(2)}, u32[]{:S(2)}) collective-permute-start(f32[8,8,128]{2,1,0:T(8,128)S(1)} %get-tuple-element.201), channel_id=1, source_target_pairs={{0,16},{1,17},{2,18},{3,19},{4,20},{5,21},{6,22},{7,23},{8,24},{9,... | collective-permute-start | bytes 98312 | tf_op jit(solution)/shard_map/ppermute | solution.py:867
  144.2 3.6 %collective-permute-start.29 = (f32[8,8,128]{2,1,0:T(8,128)S(1)}, f32[8,8,128]{2,1,0:T(8,128)S(1)}, u32[]{:S(2)}, u32[]{:S(2)}) collective-permute-start(f32[8,8,128]{2,1,0:T(8,128)S(1)} %get-tuple-element.202), channel_id=1, source_target_pairs={{0,1},{1,0},{2,3},{3,2},{4,5},{5,4},{6,7},{7,6},{8,9},{9,8},{10,11... | collective-permute-start | bytes 98312 | tf_op jit(solution)/shard_map/ppermute | solution.py:867
  144.8 3.4 %collective-permute-start.30 = (f32[8,8,128]{2,1,0:T(8,128)S(1)}, f32[8,8,128]{2,1,0:T(8,128)S(1)}, u32[]{:S(2)}, u32[]{:S(2)}) collective-permute-start(f32[8,8,128]{2,1,0:T(8,128)S(1)} %get-tuple-element.203), channel_id=1, source_target_pairs={{0,1},{1,0},{2,3},{3,2},{4,5},{5,4},{6,7},{7,6},{8,9},{9,8},{10,11... | collective-permute-start | bytes 98312 | tf_op jit(solution)/shard_map/ppermute | solution.py:867
  149.3 4.5 %collective-permute-start.32 = (f32[8,8,128]{2,1,0:T(8,128)S(1)}, f32[8,8,128]{2,1,0:T(8,128)S(1)}, u32[]{:S(2)}, u32[]{:S(2)}) collective-permute-start(f32[8,8,128]{2,1,0:T(8,128)S(1)} %get-tuple-element.214), channel_id=1, source_target_pairs={{0,16},{1,17},{2,18},{3,19},{4,20},{5,21},{6,22},{7,23},{8,24},{9,... | collective-permute-start | bytes 98312 | tf_op jit(solution)/shard_map/ppermute | solution.py:867
  150.1 3.6 %collective-permute-start.33 = (f32[8,8,128]{2,1,0:T(8,128)S(1)}, f32[8,8,128]{2,1,0:T(8,128)S(1)}, u32[]{:S(2)}, u32[]{:S(2)}) collective-permute-start(f32[8,8,128]{2,1,0:T(8,128)S(1)} %get-tuple-element.215), channel_id=1, source_target_pairs={{0,1},{1,0},{2,3},{3,2},{4,5},{5,4},{6,7},{7,6},{8,9},{9,8},{10,11... | collective-permute-start | bytes 98312 | tf_op jit(solution)/shard_map/ppermute | solution.py:867
  180.2 23.1 %all-to-all-start.5 = ((f32[128,16,128]{2,1,0:T(8,128)}), f32[128,16,128]{2,1,0:T(8,128)S(1)}, u32[]{:S(2)}, u32[]{:S(2)}) async-start(f32[128,16,128]{2,1,0:T(8,128)} %bitcast.18), calls=%async_computation.5 | async-start | bytes 2097152 | tf_op jit(solution)/shard_map/all_to_all | solution.py:879
  (14 other events, 33.5 us)

commit v2 on v1

--- a/solution.py
+++ b/solution.py
@@ -147,57 +147,91 @@
     return jnp.swapaxes(jnp.stack(out, axis=0), 0, 1)
 
 
-def local_operator(z_ref, f_ref, nb_ref, even, msgs):
+def apply_ends(v, mat):
+    s = d = None
+    for a in range(4):
+        p = float(0.5 * (mat[0, a] + mat[0, 7 - a])) * (v[a] + v[7 - a])
+        m = float(0.5 * (mat[0, a] - mat[0, 7 - a])) * (v[a] - v[7 - a])
+        s, d = (p, m) if s is None else (s + p, d + m)
+    return s + d, s - d
+
+
+def local_operator(z_ref, nb_ref, f_ref):
     wk = kvec(W)
     kt, ct = nb_ref[4], nb_ref[13]
     kw, cw = kt * wk, ct * wk
-    w0 = W[0]
-    xc = {}
     for j in range(8):
         out = apply1d([z_ref[i, j] for i in range(8)], K_)
         kwj = kw * W[j]
         res = [kwj * out[i] for i in range(8)]
         for i in range(8):
             f_ref[i, j] = res[i]
-        if j in (0, E):
-            xc[0, j], xc[E, j] = out[0], out[E]
     for i in range(8):
         block = z_ref[i]
-        v = [block[j] for j in range(8)]
         fx = [f_ref[i, j] for j in range(8)]
-        zs = apply1d(v, K_)
+        zs = apply1d([block[j] for j in range(8)], K_)
         ys = aisle_stiffness(block)
         kwi = kw * W[i]
         res = [
-            fx[j] + kwi * zs[j] + (W[i] * W[j]) * (kt * ys[j] + cw * v[j]) for j in range(8)
+            fx[j] + kwi * zs[j] + (W[i] * W[j]) * (kt * ys[j] + cw * block[j]) for j in range(8)
         ]
         for j in range(8):
             f_ref[i, j] = res[j]
-        low, high = res[0], res[E]
-        if i in (0, E):
-            kn = nb_ref[1 if i == 0 else 7] * (w0 * wk)
-            low, high = low + kn * zs[0], high + kn * zs[E]
-            for j in (0, E):
-                n = 3 if j == 0 else 5
-                res[j] = (
-                    res[j]
-                    + nb_ref[n] * (w0 * wk * xc[i, j] + (w0 * w0) * ys[j])
-                    + nb_ref[9 + n] * ((w0 * w0) * wk * v[j])
-                )
-            up, down = (1, 0) if i == 0 else (0, 1)
-
-            @pl.when(even[0])
-            def _(res=res, to=up):
-                for j in range(8):
-                    msgs[to][j] = res[j]
-
-            @pl.when(jnp.logical_not(even[0]))
-            def _(res=res, to=down):
-                for j in range(8):
-                    msgs[to][j] = res[j]
-
-        msgs[2][i] = jnp.where(even[1], high, low)
-        msgs[3][i] = jnp.where(even[1], low, high)
+
+
+def face_messages(z_ref, nb_ref, even, msgs):
+    wk = kvec(W)
+    kt, ct = nb_ref[4], nb_ref[13]
+    kw, cw = kt * wk, ct * wk
+    w0 = W[0]
+    w00 = w0 * w0
+    ends = [apply_ends([z_ref[i, j] for i in range(8)], K_) for j in range(8)]
+    for n, i in enumerate((0, E)):
+        block = z_ref[i]
+        zs, ys = apply1d([block[j] for j in range(8)], K_), aisle_stiffness(block)
+        res = [
+            kw * (W[j] * ends[j][n] + w0 * zs[j]) + (w0 * W[j]) * (kt * ys[j] + cw * block[j])
+            for j in range(8)
+        ]
+        for j, m in ((0, 3), (E, 5)):
+            res[j] = (
+                res[j]
+                + nb_ref[m] * (w0 * wk * ends[j][n] + w00 * ys[j])
+                + nb_ref[9 + m] * (w00 * wk * block[j])
+            )
+        up, down = (1, 0) if i == 0 else (0, 1)
+
+        @pl.when(even[0])
+        def _(res=res, to=up):
+            for j in range(8):
+                msgs[to][j] = res[j]
+
+        @pl.when(jnp.logical_not(even[0]))
+        def _(res=res, to=down):
+            for j in range(8):
+                msgs[to][j] = res[j]
+
+    ends = [apply_ends([z_ref[i, j] for j in range(8)], K_) for i in range(8)]
+    for n, j in enumerate((0, E)):
+        block = z_ref[:, j]
+        xs, ys = apply1d([block[i] for i in range(8)], K_), aisle_stiffness(block)
+        res = [
+            kw * (w0 * xs[i] + W[i] * ends[i][n]) + (W[i] * w0) * (kt * ys[i] + cw * block[i])
+            for i in range(8)
+        ]
+        for i, m in ((0, 1), (E, 7)):
+            res[i] = res[i] + nb_ref[m] * (w0 * wk * ends[i][n])
+        up, down = (3, 2) if j == 0 else (2, 3)
+
+        @pl.when(even[1])
+        def _(res=res, to=up):
+            for i in range(8):
+                msgs[to][i] = res[i]
+
+        @pl.when(jnp.logical_not(even[1]))
+        def _(res=res, to=down):
+            for i in range(8):
+                msgs[to][i] = res[i]
 
 
 def thomas(cf_ref, rhs):
@@ -429,14 +463,14 @@
     put_pair(even[0], f[0], f[E], (ma, mb))
 
 
-def heat_z_kernel(pos, f, ra, rb, out, ma, mb):
+def heat_z_kernel(pos, f, rb, ra, out, ma, mb):
     _, _, has, _, even = place(pos)
     out[...] = f[...]
     add_faces_x(out, (ra, rb), has, even)
     put_pair(even[1], out[:, 0], out[:, E], (ma, mb))
 
 
-def first_rows_kernel(pos, f, ra, rb, both, out, rows):
+def first_rows_kernel(pos, f, rb, ra, both, out, rows):
     _, _, has, frac, even = place(pos)
     out[...] = f[...]
     add_faces_z(out, (ra, rb), has, even)
@@ -449,7 +483,7 @@
 
 
 def setup_kernel(
-    pos, got, r, kc, cc, cf, rc, nb, dinv, z, f, m0, m1, m2, m3, c_tmp
+    pos, got, r, kc, cc, cf, rc, nb, dinv, z, m0, m1, m2, m3, c_tmp
 ):
     ix, iz, has, frac, even = place(pos)
     k_all, c_all, r_all = (coarse_rows_of(got, n) for n in range(3))
@@ -498,18 +532,18 @@
     for h in range(NZ):
         c_tmp[h] = solved[h]
     make_z(c_tmp, ix, iz, r, dinv, z)
-    local_operator(z, f, nb, even, (m0, m1, m2, m3))
-
-
-def inner_kernel(pos, f, r0, r1, r2, r3, nb, dinv, *refs):
-    w1, t, f2, m0, m1, m2, m3 = refs[-7:]
+    face_messages(z, nb, even, (m0, m1, m2, m3))
+
+
+def inner_kernel(pos, f, r3, r1, r2, r0, nb, dinv, *refs):
+    w1, t, m0, m1, m2, m3 = refs[-6:]
     _, _, has, _, even = place(pos)
     w1[...] = f[...]
     add_faces_x(w1, (r0, r1), has, even)
     add_faces_z(w1, (r2, r3), has, even)
     assemble_aisle(w1)
     t[...] = w1[...] * dinv[...]
-    local_operator(t, f2, nb, even, (m0, m1, m2, m3))
+    face_messages(t, nb, even, (m0, m1, m2, m3))
 
 
 def dots_kernel(first, *refs):
@@ -534,9 +568,9 @@
 
 def rows_kernel(first, *refs):
     if first:
-        pos, f2, r0, r1, r2, r3, t, lines, owners, v, rows = refs
+        pos, f2, r3, r1, r2, r0, t, lines, owners, v, rows = refs
     else:
-        pos, f2, r0, r1, r2, r3, t, lines, v, rows = refs
+        pos, f2, r3, r1, r2, r0, t, lines, v, rows = refs
     _, _, has, frac, even = place(pos)
     v[...] = f2[...]
     add_faces_x(v, (r0, r1), has, even)
@@ -617,7 +651,7 @@
     s1 = s2 = rs = wp = None
     if not first:
         s1, s2, rs, wp = take(4)
-    ro, rco, zo, fo, m0, m1, m2, m3, co, ay, pdo, qo = take(12)
+    ro, rco, zo, m0, m1, m2, m3, co, ay, pdo, qo = take(11)
     c_tmp, tmp = take(2)
     ix, iz, has, frac, even = place(pos)
     d = thomas(cf, coarse_rows_of(got, 0))
@@ -651,7 +685,7 @@
     for h in range(NZ):
         c_tmp[h] = solved[h]
     make_z(c_tmp, ix, iz, ro, dinv, zo)
-    local_operator(zo, fo, nb, even, (m0, m1, m2, m3))
+    face_messages(zo, nb, even, (m0, m1, m2, m3))
 
 
 def new_x(first, a1, a2, x1, x2, z, t, pd, p1, p2, x, out):
@@ -819,13 +853,10 @@
     acc = None
     step = 512
     for s in range(0, got.shape[0], step):
-        hi, lo = split(got[s : s + step])
-        hot = hot_t[:, s : s + step]
-        term = jnp.dot(hot, hi, preferred_element_type=F32) + jnp.dot(
-            hot, lo, preferred_element_type=F32
-        )
+        both = jnp.concatenate(split(got[s : s + step]), axis=1)
+        term = jnp.dot(hot_t[:, s : s + step], both, preferred_element_type=F32)
         acc = term if acc is None else acc + term
-    out[...] = acc.T
+    out[...] = (acc[:, :NY] + acc[:, NY:]).T
 
 
 def call(body, name, outs, args, scratch=()):
@@ -875,6 +906,11 @@
     return swap(pair, 1)
 
 
+def halo(msgs):
+    got = swap_x(msgs[:2]) + swap_z(msgs[2:])
+    return [got[n] for n in (3, 1, 2, 0)]
+
+
 def everywhere(rows):
     return lax.all_to_all(rows, ("row", "height"), split_axis=0, concat_axis=0, tiled=True)
 
@@ -892,33 +928,35 @@
         [((devices * SLOTS, 6 * NY), jnp.bfloat16), (devices, 128)],
         [ints],
     )
-    f, ma, mb = call(heat_z_kernel, "heat_z", [FIELD, FACE, FACE], [pos, f, ra, rb])
+    f, ma, mb = call(heat_z_kernel, "heat_z", [FIELD, FACE, FACE], [pos, f, rb, ra])
     ra, rb = swap_z((ma, mb))
     r, rows = call(
         first_rows_kernel,
         "first_rows",
         [FIELD, (devices, 4, NY)],
-        [pos, f, ra, rb, both],
+        [pos, f, rb, ra, both],
     )
     got0 = everywhere(rows).reshape(devices * 4, NY)
-    kc, cc, cf, rc, nb, dinv, z, f, *msgs = call(
+    kc, cc, cf, rc, nb, dinv, z, *msgs = call(
         setup_kernel,
         "setup",
-        [COARSE, COARSE, (48, NX, NY), COARSE, (18, 8, NY), FIELD, FIELD, FIELD] + [FACE] * 4,
+        [COARSE, COARSE, (48, NX, NY), COARSE, (18, 8, NY), FIELD, FIELD] + [FACE] * 4,
         [pos, got0, r],
         scratch=[COARSE],
     )
     x = p1 = p2 = s1 = s2 = rs = co = None
     for outer in range(ITERS // 2):
         first, last = outer == 0, outer == ITERS // 2 - 1
-        got = swap_x(msgs[:2]) + swap_z(msgs[2:])
-        w1, t, f2, *msgs = call(
+        got = halo(msgs)
+        (f,) = call(local_operator, "apply", [FIELD], [z, nb])
+        w1, t, *msgs = call(
             inner_kernel,
             "inner",
-            [FIELD] * 3 + [FACE] * 4,
+            [FIELD] * 2 + [FACE] * 4,
             [pos, f, *got, nb, dinv] + ([] if first else [rs]),
         )
-        got = swap_x(msgs[:2]) + swap_z(msgs[2:])
+        got = halo(msgs)
+        (f2,) = call(local_operator, "apply", [FIELD], [t, nb])
         (lines,) = call(
             functools.partial(dots_kernel, first),
             "dots",
@@ -938,10 +976,10 @@
             )
         if last:
             break
-        rn, rcn, zn, f, *msgs, con, ay, pd, q = call(
+        rn, rcn, zn, *msgs, con, ay, pd, q = call(
             functools.partial(step_kernel, first),
             "step",
-            [FIELD, COARSE, FIELD, FIELD]
+            [FIELD, COARSE, FIELD]
             + [FACE] * 4
             + [(9, 8, NY), FIELD, (9, 8, NY), COARSE],
             [pos, rows, r, w1, v, dinv, nb, kc, cc, cf, rc] + ([] if first else [s1, s2, rs, co]),

time: 205 us -> 194 us (0.946)
  blocking collectives: 107 us -> 95 us
  starting transfers between devices: 36.3 us -> 38.5 us
  waiting for transfers between devices: 26 us -> 23.8 us
    all_to_all x5, blocking collectives: 107 us -> 95 us  [everywhere(): lax.all_to_all(rows, ('row', 'height'), split_axis=0, concat_axis=0, tile...]
    ppermute x36, starting transfers between devices: 32.1 us -> 34.3 us  [swap(): lax.ppermute(v, ('row', 'height'), pairs(axis, n == 1))]
    ppermute x36, waiting for transfers between devices: 9.23 us -> 7.07 us  [swap(): lax.ppermute(v, ('row', 'height'), pairs(axis, n == 1))]
    pallas_call x27 -> x35, Pallas kernels: 31.3 us -> 32.9 us  [call(): pl.pallas_call(body, out_shape=[jax.ShapeDtypeStruct(*shape(o)) for o in...]
  transfers between devices with their start and end apart: 37 -> 37, of which waited for: 15 -> 12; matrix products, arithmetic and copies ran while one was open for 1% -> 1% of each run, Pallas kernels for 4% -> 6%
where the time goes in v2:
time: 194 us
  blocking collectives  95 us (49%)
  starting transfers between devices  38.5 us (20%)
  Pallas kernels  32.9 us (17%)
  waiting for transfers between devices  23.8 us (12%)
    all_to_all x5, blocking collectives, everywhere(): lax.all_to_all(rows, ('row', 'height'), split_axis=0, concat_axis=0, tile...  95 us
    ppermute x36, starting transfers between devices, swap(): lax.ppermute(v, ('row', 'height'), pairs(axis, n == 1))  34.3 us
    pallas_call x35, Pallas kernels, call(): pl.pallas_call(body, out_shape=[jax.ShapeDtypeStruct(*shape(o)) for o in...  32.9 us
    all_to_all x1, waiting for transfers between devices, everywhere(): lax.all_to_all(rows, ('row', 'height'), split_axis=0, concat_axis=0, tile...  16.8 us
    ppermute x36, waiting for transfers between devices, swap(): lax.ppermute(v, ('row', 'height'), pairs(axis, n == 1))  7.07 us
    all_to_all x1, starting transfers between devices, everywhere(): lax.all_to_all(rows, ('row', 'height'), split_axis=0, concat_axis=0, tile...  4.19 us
  transfers between devices with their start and end apart: 37, of which 12 were waited for; matrix products, arithmetic and copies ran while one was open for 1% of the time, Pallas kernels for 6%

profile of v2, /device:TPU:1, one launch (start us, length us, event | category | flops | bytes accessed | tf_op | source)
XLA Modules:
  0.0 193.6 jit_solution(11968129825229386071)
XLA Ops:
  2.3 3.1 %collective-permute-start = (f32[8,8,128]{2,1,0:T(8,128)S(1)}, f32[8,8,128]{2,1,0:T(8,128)S(1)}, u32[]{:S(2)}, u32[]{:S(2)}) collective-permute-start(f32[8,8,128]{2,1,0:T(8,128)S(1)} %get-tuple-element.112), channel_id=1, source_target_pairs={{0,1},{1,0},{2,3},{3,2},{4,5},{5,4},{6,7},{7,6},{8,9},{9,8},{10,11... | collective-permute-start | bytes 98312 | tf_op jit(solution)/shard_map/ppermute | solution.py:898
  8.4 2.0 %collective-permute-start.3 = (f32[8,8,128]{2,1,0:T(8,128)S(1)}, f32[8,8,128]{2,1,0:T(8,128)S(1)}, u32[]{:S(2)}, u32[]{:S(2)}) collective-permute-start(f32[8,8,128]{2,1,0:T(8,128)S(1)} %get-tuple-element.116), channel_id=1, source_target_pairs={{0,1},{1,0},{2,3},{3,2},{4,5},{5,4},{6,7},{7,6},{8,9},{9,8},{10,11... | collective-permute-start | bytes 98312 | tf_op jit(solution)/shard_map/ppermute | solution.py:898
  12.4 23.0 %all_to_all.30 = f32[128,4,128]{2,1,0:T(4,128)S(1)} all-to-all(f32[128,4,128]{2,1,0:T(4,128)S(1)} %get-tuple-element.117), channel_id=1, replica_groups=mesh['row'=8,'height'=16] {'row','height'}, dimensions={0} | all-to-all | bytes 524288 | tf_op jit(solution)/shard_map/all_to_all | solution.py:915
  35.4 1.3 setup.1
  42.8 1.8 collective-permute-start.11
  44.9 1.5 slots.1
  48.7 18.8 %all_to_all.31 = f32[128,4,128]{2,1,0:T(4,128)S(1)} all-to-all(f32[128,4,128]{2,1,0:T(4,128)S(1)} %get-tuple-element.133), channel_id=1, replica_groups=mesh['row'=8,'height'=16] {'row','height'}, dimensions={0} | all-to-all | bytes 524288 | tf_op jit(solution)/shard_map/all_to_all | solution.py:915
  67.5 2.4 %step.3 = (f32[8,8,8,128]{3,2,1,0:T(8,128)S(1)}, f32[16,8,128]{2,1,0:T(8,128)S(1)}, f32[8,8,8,128]{3,2,1,0:T(8,128)S(1)}, f32[8,8,128]{2,1,0:T(8,128)S(1)}, f32[...) custom-call(s32[2]{0:T(128)S(1)} %pad_add_fusion.1.pos.refs_0_, ...), custom_call_target="tpu_custom_call" | custom-call | flops 2000000 | bytes 1048576 | tf_op jit(solution)/shard_map/step/pallas_call | solution.py:867
  77.5 1.3 collective-permute-start.18
  78.8 1.6 collective-permute-start.19
  82.4 17.7 %all_to_all.32 = f32[128,4,128]{2,1,0:T(4,128)S(1)} all-to-all(f32[128,4,128]{2,1,0:T(4,128)S(1)} %get-tuple-element.158), channel_id=1, replica_groups=mesh['row'=8,'height'=16] {'row','height'}, dimensions={0} | all-to-all | bytes 524288 | tf_op jit(solution)/shard_map/all_to_all | solution.py:915
  100.1 2.4 %step.4 = (f32[8,8,8,128]{3,2,1,0:T(8,128)S(1)}, f32[16,8,128]{2,1,0:T(8,128)S(1)}, f32[8,8,8,128]{3,2,1,0:T(8,128)S(1)}, f32[8,8,128]{2,1,0:T(8,128)S(1)}, f32[...) custom-call(s32[2]{0:T(128)S(1)} %pad_add_fusion.1.pos.refs_0_, ...), custom_call_target="tpu_custom_call" | custom-call | flops 2000000 | bytes 1048576 | tf_op jit(solution)/shard_map/step/pallas_call | solution.py:867
  104.1 1.3 collective-permute-start.23
  110.1 1.3 collective-permute-start.26
  111.4 1.6 collective-permute-start.27
  115.0 17.7 %all_to_all.33 = f32[128,4,128]{2,1,0:T(4,128)S(1)} all-to-all(f32[128,4,128]{2,1,0:T(4,128)S(1)} %get-tuple-element.183), channel_id=1, replica_groups=mesh['row'=8,'height'=16] {'row','height'}, dimensions={0} | all-to-all | bytes 524288 | tf_op jit(solution)/shard_map/all_to_all | solution.py:915
  132.7 2.4 %step.5 = (f32[8,8,8,128]{3,2,1,0:T(8,128)S(1)}, f32[16,8,128]{2,1,0:T(8,128)S(1)}, f32[8,8,8,128]{3,2,1,0:T(8,128)S(1)}, f32[8,8,128]{2,1,0:T(8,128)S(1)}, f32[...) custom-call(s32[2]{0:T(128)S(1)} %pad_add_fusion.1.pos.refs_0_, ...), custom_call_target="tpu_custom_call" | custom-call | flops 2000000 | bytes 1048576 | tf_op jit(solution)/shard_map/step/pallas_call | solution.py:867
  142.9 1.3 collective-permute-start.34
  144.2 1.6 collective-permute-start.35
  147.8 17.7 %all_to_all.34 = f32[128,4,128]{2,1,0:T(4,128)S(1)} all-to-all(f32[128,4,128]{2,1,0:T(4,128)S(1)} %get-tuple-element.208), channel_id=1, replica_groups=mesh['row'=8,'height'=16] {'row','height'}, dimensions={0} | all-to-all | bytes 524288 | tf_op jit(solution)/shard_map/all_to_all | solution.py:915
  165.5 4.0 %last.1 = (f32[8,8,8,128]{3,2,1,0:T(8,128)}, f32[2048,128]{1,0:T(8,128)}, f32[4,8,128]{2,1,0:T(8,128)S(1)}, f32[16,8,128]{2,1,0:T(8,128)S(1)}) custom-call(s32[2]{0:T(128)S(1)} %pad_add_fusion.1.pos.refs_0_, f32[512,128]{1,0:T(8,128)S(1)} %bitcast.34, f32[8,8,8,128]{3,2,1,0:T(8,128)S(1)} %get-tuple-element.186.z_ref.refs_1_.z, ...), custom_call_target="tpu_custom_call" | custom-call | flops 2000000 | bytes 1048576 | tf_op jit(solution)/shard_map/last/pallas_call | solution.py:867
  169.6 4.2 %all-to-all-start.5 = ((f32[128,16,128]{2,1,0:T(8,128)}), f32[128,16,128]{2,1,0:T(8,128)S(1)}, u32[]{:S(2)}, u32[]{:S(2)}) async-start(f32[128,16,128]{2,1,0:T(8,128)} %bitcast.18), calls=%async_computation.5 | async-start | bytes 2097152 | tf_op jit(solution)/shard_map/all_to_all | solution.py:915
  174.2 1.7 residual.1
  175.9 16.8 %all-to-all-done.5 = f32[128,16,128]{2,1,0:T(8,128)S(1)} async-done(((f32[128,16,128]{2,1,0:T(8,128)}), f32[128,16,128]{2,1,0:T(8,128)S(1)}, u32[]{:S(2)}, u32[]{:S(2)}) %all-to-all-start.5) | async-done | bytes 1048608 | tf_op jit(solution)/shard_map/all_to_all | solution.py:915
  (104 shorter events, 44.0 us)
Async XLA Ops:
  2.3 5.0 %collective-permute-start = (f32[8,8,128]{2,1,0:T(8,128)S(1)}, f32[8,8,128]{2,1,0:T(8,128)S(1)}, u32[]{:S(2)}, u32[]{:S(2)}) collective-permute-start(f32[8,8,128]{2,1,0:T(8,128)S(1)} %get-tuple-element.112), channel_id=1, source_target_pairs={{0,1},{1,0},{2,3},{3,2},{4,5},{5,4},{6,7},{7,6},{8,9},{9,8},{10,11... | collective-permute-start | bytes 98312 | tf_op jit(solution)/shard_map/ppermute | solution.py:898
  37.5 3.6 %collective-permute-start.5 = (f32[8,8,128]{2,1,0:T(8,128)S(1)}, f32[8,8,128]{2,1,0:T(8,128)S(1)}, u32[]{:S(2)}, u32[]{:S(2)}) collective-permute-start(f32[8,8,128]{2,1,0:T(8,128)S(1)} %get-tuple-element.122), channel_id=1, source_target_pairs={{0,1},{1,0},{2,3},{3,2},{4,5},{5,4},{6,7},{7,6},{8,9},{9,8},{10,11... | collective-permute-start | bytes 98312 | tf_op jit(solution)/shard_map/ppermute | solution.py:898
  38.0 3.4 %collective-permute-start.6 = (f32[8,8,128]{2,1,0:T(8,128)S(1)}, f32[8,8,128]{2,1,0:T(8,128)S(1)}, u32[]{:S(2)}, u32[]{:S(2)}) collective-permute-start(f32[8,8,128]{2,1,0:T(8,128)S(1)} %get-tuple-element.123), channel_id=1, source_target_pairs={{0,1},{1,0},{2,3},{3,2},{4,5},{5,4},{6,7},{7,6},{8,9},{9,8},{10,11... | collective-permute-start | bytes 98312 | tf_op jit(solution)/shard_map/ppermute | solution.py:898
  42.4 5.1 %collective-permute-start.10 = (f32[8,8,128]{2,1,0:T(8,128)S(1)}, f32[8,8,128]{2,1,0:T(8,128)S(1)}, u32[]{:S(2)}, u32[]{:S(2)}) collective-permute-start(f32[8,8,128]{2,1,0:T(8,128)S(1)} %get-tuple-element.129), channel_id=1, source_target_pairs={{0,1},{1,0},{2,3},{3,2},{4,5},{5,4},{6,7},{7,6},{8,9},{9,8},{10,11... | collective-permute-start | bytes 98312 | tf_op jit(solution)/shard_map/ppermute | solution.py:898
  42.8 4.7 %collective-permute-start.11 = (f32[8,8,128]{2,1,0:T(8,128)S(1)}, f32[8,8,128]{2,1,0:T(8,128)S(1)}, u32[]{:S(2)}, u32[]{:S(2)}) collective-permute-start(f32[8,8,128]{2,1,0:T(8,128)S(1)} %get-tuple-element.130), channel_id=1, source_target_pairs={{0,16},{1,17},{2,18},{3,19},{4,20},{5,21},{6,22},{7,23},{8,24},{9,... | collective-permute-start | bytes 98312 | tf_op jit(solution)/shard_map/ppermute | solution.py:898
  69.9 3.5 %collective-permute-start.12 = (f32[8,8,128]{2,1,0:T(8,128)S(1)}, f32[8,8,128]{2,1,0:T(8,128)S(1)}, u32[]{:S(2)}, u32[]{:S(2)}) collective-permute-start(f32[8,8,128]{2,1,0:T(8,128)S(1)} %get-tuple-element.140), channel_id=1, source_target_pairs={{0,16},{1,2},{2,1},{3,4},{4,3},{5,6},{6,5},{7,8},{8,7},{9,10},{10,... | collective-permute-start | bytes 98312 | tf_op jit(solution)/shard_map/ppermute | solution.py:898
  70.7 3.6 %collective-permute-start.13 = (f32[8,8,128]{2,1,0:T(8,128)S(1)}, f32[8,8,128]{2,1,0:T(8,128)S(1)}, u32[]{:S(2)}, u32[]{:S(2)}) collective-permute-start(f32[8,8,128]{2,1,0:T(8,128)S(1)} %get-tuple-element.141), channel_id=1, source_target_pairs={{0,1},{1,0},{2,3},{3,2},{4,5},{5,4},{6,7},{7,6},{8,9},{9,8},{10,11... | collective-permute-start | bytes 98312 | tf_op jit(solution)/shard_map/ppermute | solution.py:898
  71.2 3.4 %collective-permute-start.14 = (f32[8,8,128]{2,1,0:T(8,128)S(1)}, f32[8,8,128]{2,1,0:T(8,128)S(1)}, u32[]{:S(2)}, u32[]{:S(2)}) collective-permute-start(f32[8,8,128]{2,1,0:T(8,128)S(1)} %get-tuple-element.142), channel_id=1, source_target_pairs={{0,1},{1,0},{2,3},{3,2},{4,5},{5,4},{6,7},{7,6},{8,9},{9,8},{10,11... | collective-permute-start | bytes 98312 | tf_op jit(solution)/shard_map/ppermute | solution.py:898
  75.6 6.0 %collective-permute-start.16 = (f32[8,8,128]{2,1,0:T(8,128)S(1)}, f32[8,8,128]{2,1,0:T(8,128)S(1)}, u32[]{:S(2)}, u32[]{:S(2)}) collective-permute-start(f32[8,8,128]{2,1,0:T(8,128)S(1)} %get-tuple-element.150), channel_id=1, source_target_pairs={{0,16},{1,2},{2,1},{3,4},{4,3},{5,6},{6,5},{7,8},{8,7},{9,10},{10,... | collective-permute-start | bytes 98312 | tf_op jit(solution)/shard_map/ppermute | solution.py:898
  76.4 5.2 %collective-permute-start.17 = (f32[8,8,128]{2,1,0:T(8,128)S(1)}, f32[8,8,128]{2,1,0:T(8,128)S(1)}, u32[]{:S(2)}, u32[]{:S(2)}) collective-permute-start(f32[8,8,128]{2,1,0:T(8,128)S(1)} %get-tuple-element.151), channel_id=1, source_target_pairs={{0,1},{1,0},{2,3},{3,2},{4,5},{5,4},{6,7},{7,6},{8,9},{9,8},{10,11... | collective-permute-start | bytes 98312 | tf_op jit(solution)/shard_map/ppermute | solution.py:898
  77.5 4.1 %collective-permute-start.18 = (f32[8,8,128]{2,1,0:T(8,128)S(1)}, f32[8,8,128]{2,1,0:T(8,128)S(1)}, u32[]{:S(2)}, u32[]{:S(2)}) collective-permute-start(f32[8,8,128]{2,1,0:T(8,128)S(1)} %get-tuple-element.152), channel_id=1, source_target_pairs={{0,1},{1,0},{2,3},{3,2},{4,5},{5,4},{6,7},{7,6},{8,9},{9,8},{10,11... | collective-permute-start | bytes 98312 | tf_op jit(solution)/shard_map/ppermute | solution.py:898
  102.5 3.6 %collective-permute-start.20 = (f32[8,8,128]{2,1,0:T(8,128)S(1)}, f32[8,8,128]{2,1,0:T(8,128)S(1)}, u32[]{:S(2)}, u32[]{:S(2)}) collective-permute-start(f32[8,8,128]{2,1,0:T(8,128)S(1)} %get-tuple-element.162), channel_id=1, source_target_pairs={{0,16},{1,2},{2,1},{3,4},{4,3},{5,6},{6,5},{7,8},{8,7},{9,10},{10,... | collective-permute-start | bytes 98312 | tf_op jit(solution)/shard_map/ppermute | solution.py:898
  103.3 3.6 %collective-permute-start.21 = (f32[8,8,128]{2,1,0:T(8,128)S(1)}, f32[8,8,128]{2,1,0:T(8,128)S(1)}, u32[]{:S(2)}, u32[]{:S(2)}) collective-permute-start(f32[8,8,128]{2,1,0:T(8,128)S(1)} %get-tuple-element.163), channel_id=1, source_target_pairs={{0,1},{1,0},{2,3},{3,2},{4,5},{5,4},{6,7},{7,6},{8,9},{9,8},{10,11... | collective-permute-start | bytes 98312 | tf_op jit(solution)/shard_map/ppermute | solution.py:898
  103.8 3.4 %collective-permute-start.22 = (f32[8,8,128]{2,1,0:T(8,128)S(1)}, f32[8,8,128]{2,1,0:T(8,128)S(1)}, u32[]{:S(2)}, u32[]{:S(2)}) collective-permute-start(f32[8,8,128]{2,1,0:T(8,128)S(1)} %get-tuple-element.164), channel_id=1, source_target_pairs={{0,1},{1,0},{2,3},{3,2},{4,5},{5,4},{6,7},{7,6},{8,9},{9,8},{10,11... | collective-permute-start | bytes 98312 | tf_op jit(solution)/shard_map/ppermute | solution.py:898
  108.2 6.1 %collective-permute-start.24 = (f32[8,8,128]{2,1,0:T(8,128)S(1)}, f32[8,8,128]{2,1,0:T(8,128)S(1)}, u32[]{:S(2)}, u32[]{:S(2)}) collective-permute-start(f32[8,8,128]{2,1,0:T(8,128)S(1)} %get-tuple-element.175), channel_id=1, source_target_pairs={{0,16},{1,2},{2,1},{3,4},{4,3},{5,6},{6,5},{7,8},{8,7},{9,10},{10,... | collective-permute-start | bytes 98312 | tf_op jit(solution)/shard_map/ppermute | solution.py:898
  109.0 5.2 %collective-permute-start.25 = (f32[8,8,128]{2,1,0:T(8,128)S(1)}, f32[8,8,128]{2,1,0:T(8,128)S(1)}, u32[]{:S(2)}, u32[]{:S(2)}) collective-permute-start(f32[8,8,128]{2,1,0:T(8,128)S(1)} %get-tuple-element.176), channel_id=1, source_target_pairs={{0,1},{1,0},{2,3},{3,2},{4,5},{5,4},{6,7},{7,6},{8,9},{9,8},{10,11... | collective-permute-start | bytes 98312 | tf_op jit(solution)/shard_map/ppermute | solution.py:898
  110.1 4.2 %collective-permute-start.26 = (f32[8,8,128]{2,1,0:T(8,128)S(1)}, f32[8,8,128]{2,1,0:T(8,128)S(1)}, u32[]{:S(2)}, u32[]{:S(2)}) collective-permute-start(f32[8,8,128]{2,1,0:T(8,128)S(1)} %get-tuple-element.177), channel_id=1, source_target_pairs={{0,1},{1,0},{2,3},{3,2},{4,5},{5,4},{6,7},{7,6},{8,9},{9,8},{10,11... | collective-permute-start | bytes 98312 | tf_op jit(solution)/shard_map/ppermute | solution.py:898
  135.1 3.9 %collective-permute-start.28 = (f32[8,8,128]{2,1,0:T(8,128)S(1)}, f32[8,8,128]{2,1,0:T(8,128)S(1)}, u32[]{:S(2)}, u32[]{:S(2)}) collective-permute-start(f32[8,8,128]{2,1,0:T(8,128)S(1)} %get-tuple-element.187), channel_id=1, source_target_pairs={{0,16},{1,2},{2,1},{3,4},{4,3},{5,6},{6,5},{7,8},{8,7},{9,10},{10,... | collective-permute-start | bytes 98312 | tf_op jit(solution)/shard_map/ppermute | solution.py:898
  136.1 3.6 %collective-permute-start.29 = (f32[8,8,128]{2,1,0:T(8,128)S(1)}, f32[8,8,128]{2,1,0:T(8,128)S(1)}, u32[]{:S(2)}, u32[]{:S(2)}) collective-permute-start(f32[8,8,128]{2,1,0:T(8,128)S(1)} %get-tuple-element.188), channel_id=1, source_target_pairs={{0,1},{1,0},{2,3},{3,2},{4,5},{5,4},{6,7},{7,6},{8,9},{9,8},{10,11... | collective-permute-start | bytes 98312 | tf_op jit(solution)/shard_map/ppermute | solution.py:898
  136.6 3.4 %collective-permute-start.30 = (f32[8,8,128]{2,1,0:T(8,128)S(1)}, f32[8,8,128]{2,1,0:T(8,128)S(1)}, u32[]{:S(2)}, u32[]{:S(2)}) collective-permute-start(f32[8,8,128]{2,1,0:T(8,128)S(1)} %get-tuple-element.189), channel_id=1, source_target_pairs={{0,1},{1,0},{2,3},{3,2},{4,5},{5,4},{6,7},{7,6},{8,9},{9,8},{10,11... | collective-permute-start | bytes 98312 | tf_op jit(solution)/shard_map/ppermute | solution.py:898
  141.0 6.0 %collective-permute-start.32 = (f32[8,8,128]{2,1,0:T(8,128)S(1)}, f32[8,8,128]{2,1,0:T(8,128)S(1)}, u32[]{:S(2)}, u32[]{:S(2)}) collective-permute-start(f32[8,8,128]{2,1,0:T(8,128)S(1)} %get-tuple-element.200), channel_id=1, source_target_pairs={{0,16},{1,2},{2,1},{3,4},{4,3},{5,6},{6,5},{7,8},{8,7},{9,10},{10,... | collective-permute-start | bytes 98312 | tf_op jit(solution)/shard_map/ppermute | solution.py:898
  141.8 5.2 %collective-permute-start.33 = (f32[8,8,128]{2,1,0:T(8,128)S(1)}, f32[8,8,128]{2,1,0:T(8,128)S(1)}, u32[]{:S(2)}, u32[]{:S(2)}) collective-permute-start(f32[8,8,128]{2,1,0:T(8,128)S(1)} %get-tuple-element.201), channel_id=1, source_target_pairs={{0,1},{1,0},{2,3},{3,2},{4,5},{5,4},{6,7},{7,6},{8,9},{9,8},{10,11... | collective-permute-start | bytes 98312 | tf_op jit(solution)/shard_map/ppermute | solution.py:898
  142.9 4.1 %collective-permute-start.34 = (f32[8,8,128]{2,1,0:T(8,128)S(1)}, f32[8,8,128]{2,1,0:T(8,128)S(1)}, u32[]{:S(2)}, u32[]{:S(2)}) collective-permute-start(f32[8,8,128]{2,1,0:T(8,128)S(1)} %get-tuple-element.202), channel_id=1, source_target_pairs={{0,1},{1,0},{2,3},{3,2},{4,5},{5,4},{6,7},{7,6},{8,9},{9,8},{10,11... | collective-permute-start | bytes 98312 | tf_op jit(solution)/shard_map/ppermute | solution.py:898
  169.6 23.1 %all-to-all-start.5 = ((f32[128,16,128]{2,1,0:T(8,128)}), f32[128,16,128]{2,1,0:T(8,128)S(1)}, u32[]{:S(2)}, u32[]{:S(2)}) async-start(f32[128,16,128]{2,1,0:T(8,128)} %bitcast.18), calls=%async_computation.5 | async-start | bytes 2097152 | tf_op jit(solution)/shard_map/all_to_all | solution.py:915
  (18 other events, 216.5 us)

commit v3 on v2

--- a/solution.py
+++ b/solution.py
@@ -568,7 +568,7 @@
 
 def rows_kernel(first, *refs):
     if first:
-        pos, f2, r3, r1, r2, r0, t, lines, owners, v, rows = refs
+        pos, f2, r2, r0, r3, r1, t, lines, owners, v, rows = refs
     else:
         pos, f2, r3, r1, r2, r0, t, lines, v, rows = refs
     _, _, has, frac, even = place(pos)
@@ -906,9 +906,9 @@
     return swap(pair, 1)
 
 
-def halo(msgs):
+def halo(msgs, order=(3, 1, 2, 0)):
     got = swap_x(msgs[:2]) + swap_z(msgs[2:])
-    return [got[n] for n in (3, 1, 2, 0)]
+    return [got[n] for n in order]
 
 
 def everywhere(rows):
@@ -955,7 +955,7 @@
             [FIELD] * 2 + [FACE] * 4,
             [pos, f, *got, nb, dinv] + ([] if first else [rs]),
         )
-        got = halo(msgs)
+        got = halo(msgs, (2, 0, 3, 1)) if first else halo(msgs)
         (f2,) = call(local_operator, "apply", [FIELD], [t, nb])
         (lines,) = call(
             functools.partial(dots_kernel, first),

time: 194 us -> 194 us (level)
  starting transfers between devices: 38.5 us -> 40.9 us
  blocking collectives: 95 us -> 92.7 us
    ppermute x36, starting transfers between devices: 34.3 us -> 36.7 us  [swap(): lax.ppermute(v, ('row', 'height'), pairs(axis, n == 1))]
    all_to_all x5, blocking collectives: 95 us -> 92.7 us  [everywhere(): lax.all_to_all(rows, ('row', 'height'), split_axis=0, concat_axis=0, tile...]
  transfers between devices with their start and end apart: 37 -> 37, of which waited for: 12 -> 11; matrix products, arithmetic and copies ran while one was open for 1% -> 1% of each run, Pallas kernels for 6% -> 6%
where the time goes in v3:
time: 194 us; the launch traced here: 193 us
  blocking collectives  92.7 us (48%)
  starting transfers between devices  40.9 us (21%)
  Pallas kernels  32.9 us (17%)
  waiting for transfers between devices  23.4 us (12%)
    all_to_all x5, blocking collectives, everywhere(): lax.all_to_all(rows, ('row', 'height'), split_axis=0, concat_axis=0, tile...  92.7 us
    ppermute x36, starting transfers between devices, swap(): lax.ppermute(v, ('row', 'height'), pairs(axis, n == 1))  36.7 us
    pallas_call x35, Pallas kernels, call(): pl.pallas_call(body, out_shape=[jax.ShapeDtypeStruct(*shape(o)) for o in...  32.9 us
    all_to_all x1, waiting for transfers between devices, everywhere(): lax.all_to_all(rows, ('row', 'height'), split_axis=0, concat_axis=0, tile...  16.7 us
    ppermute x36, waiting for transfers between devices, swap(): lax.ppermute(v, ('row', 'height'), pairs(axis, n == 1))  6.61 us
    all_to_all x1, starting transfers between devices, everywhere(): lax.all_to_all(rows, ('row', 'height'), split_axis=0, concat_axis=0, tile...  4.2 us
  transfers between devices with their start and end apart: 37, of which 11 were waited for; matrix products, arithmetic and copies ran while one was open for 1% of the time, Pallas kernels for 6%

profile of v3, /device:TPU:1, one launch (start us, length us, event | category | flops | bytes accessed | tf_op | source)
XLA Modules:
  0.0 193.3 jit_solution(10212851492406053575)
XLA Ops:
  2.3 3.1 %collective-permute-start = (f32[8,8,128]{2,1,0:T(8,128)S(1)}, f32[8,8,128]{2,1,0:T(8,128)S(1)}, u32[]{:S(2)}, u32[]{:S(2)}) collective-permute-start(f32[8,8,128]{2,1,0:T(8,128)S(1)} %get-tuple-element.112), channel_id=1, source_target_pairs={{0,1},{1,0},{2,3},{3,2},{4,5},{5,4},{6,7},{7,6},{8,9},{9,8},{10,11... | collective-permute-start | bytes 98312 | tf_op jit(solution)/shard_map/ppermute | solution.py:898
  8.4 2.0 %collective-permute-start.3 = (f32[8,8,128]{2,1,0:T(8,128)S(1)}, f32[8,8,128]{2,1,0:T(8,128)S(1)}, u32[]{:S(2)}, u32[]{:S(2)}) collective-permute-start(f32[8,8,128]{2,1,0:T(8,128)S(1)} %get-tuple-element.116), channel_id=1, source_target_pairs={{0,1},{1,0},{2,3},{3,2},{4,5},{5,4},{6,7},{7,6},{8,9},{9,8},{10,11... | collective-permute-start | bytes 98312 | tf_op jit(solution)/shard_map/ppermute | solution.py:898
  12.4 23.0 %all_to_all.30 = f32[128,4,128]{2,1,0:T(4,128)S(1)} all-to-all(f32[128,4,128]{2,1,0:T(4,128)S(1)} %get-tuple-element.117), channel_id=1, replica_groups=mesh['row'=8,'height'=16] {'row','height'}, dimensions={0} | all-to-all | bytes 524288 | tf_op jit(solution)/shard_map/all_to_all | solution.py:915
  35.4 1.3 setup.1
  44.3 1.3 collective-permute-start.8
  45.6 1.6 collective-permute-start.9
  47.3 1.5 slots.1
  50.7 16.5 %all_to_all.31 = f32[128,4,128]{2,1,0:T(4,128)S(1)} all-to-all(f32[128,4,128]{2,1,0:T(4,128)S(1)} %get-tuple-element.133), channel_id=1, replica_groups=mesh['row'=8,'height'=16] {'row','height'}, dimensions={0} | all-to-all | bytes 524288 | tf_op jit(solution)/shard_map/all_to_all | solution.py:915
  67.2 2.4 %step.3 = (f32[8,8,8,128]{3,2,1,0:T(8,128)S(1)}, f32[16,8,128]{2,1,0:T(8,128)S(1)}, f32[8,8,8,128]{3,2,1,0:T(8,128)S(1)}, f32[8,8,128]{2,1,0:T(8,128)S(1)}, f32[...) custom-call(s32[2]{0:T(128)S(1)} %pad_add_fusion.1.pos.refs_0_, ...), custom_call_target="tpu_custom_call" | custom-call | flops 2000000 | bytes 1048576 | tf_op jit(solution)/shard_map/step/pallas_call | solution.py:867
  77.1 1.3 collective-permute-start.18
  78.4 1.6 collective-permute-start.19
  82.0 17.7 %all_to_all.32 = f32[128,4,128]{2,1,0:T(4,128)S(1)} all-to-all(f32[128,4,128]{2,1,0:T(4,128)S(1)} %get-tuple-element.158), channel_id=1, replica_groups=mesh['row'=8,'height'=16] {'row','height'}, dimensions={0} | all-to-all | bytes 524288 | tf_op jit(solution)/shard_map/all_to_all | solution.py:915
  99.7 2.4 %step.4 = (f32[8,8,8,128]{3,2,1,0:T(8,128)S(1)}, f32[16,8,128]{2,1,0:T(8,128)S(1)}, f32[8,8,8,128]{3,2,1,0:T(8,128)S(1)}, f32[8,8,128]{2,1,0:T(8,128)S(1)}, f32[...) custom-call(s32[2]{0:T(128)S(1)} %pad_add_fusion.1.pos.refs_0_, ...), custom_call_target="tpu_custom_call" | custom-call | flops 2000000 | bytes 1048576 | tf_op jit(solution)/shard_map/step/pallas_call | solution.py:867
  109.7 1.3 collective-permute-start.26
  111.0 1.6 collective-permute-start.27
  114.6 17.7 %all_to_all.33 = f32[128,4,128]{2,1,0:T(4,128)S(1)} all-to-all(f32[128,4,128]{2,1,0:T(4,128)S(1)} %get-tuple-element.183), channel_id=1, replica_groups=mesh['row'=8,'height'=16] {'row','height'}, dimensions={0} | all-to-all | bytes 524288 | tf_op jit(solution)/shard_map/all_to_all | solution.py:915
  132.3 2.4 %step.5 = (f32[8,8,8,128]{3,2,1,0:T(8,128)S(1)}, f32[16,8,128]{2,1,0:T(8,128)S(1)}, f32[8,8,8,128]{3,2,1,0:T(8,128)S(1)}, f32[8,8,128]{2,1,0:T(8,128)S(1)}, f32[...) custom-call(s32[2]{0:T(128)S(1)} %pad_add_fusion.1.pos.refs_0_, ...), custom_call_target="tpu_custom_call" | custom-call | flops 2000000 | bytes 1048576 | tf_op jit(solution)/shard_map/step/pallas_call | solution.py:867
  142.5 1.3 collective-permute-start.34
  143.8 1.6 collective-permute-start.35
  147.4 17.7 %all_to_all.34 = f32[128,4,128]{2,1,0:T(4,128)S(1)} all-to-all(f32[128,4,128]{2,1,0:T(4,128)S(1)} %get-tuple-element.208), channel_id=1, replica_groups=mesh['row'=8,'height'=16] {'row','height'}, dimensions={0} | all-to-all | bytes 524288 | tf_op jit(solution)/shard_map/all_to_all | solution.py:915
  165.2 4.0 %last.1 = (f32[8,8,8,128]{3,2,1,0:T(8,128)}, f32[2048,128]{1,0:T(8,128)}, f32[4,8,128]{2,1,0:T(8,128)S(1)}, f32[16,8,128]{2,1,0:T(8,128)S(1)}) custom-call(s32[2]{0:T(128)S(1)} %pad_add_fusion.1.pos.refs_0_, f32[512,128]{1,0:T(8,128)S(1)} %bitcast.34, f32[8,8,8,128]{3,2,1,0:T(8,128)S(1)} %get-tuple-element.186.z_ref.refs_1_.z, ...), custom_call_target="tpu_custom_call" | custom-call | flops 2000000 | bytes 1048576 | tf_op jit(solution)/shard_map/last/pallas_call | solution.py:867
  169.2 4.2 %all-to-all-start.5 = ((f32[128,16,128]{2,1,0:T(8,128)}), f32[128,16,128]{2,1,0:T(8,128)S(1)}, u32[]{:S(2)}, u32[]{:S(2)}) async-start(f32[128,16,128]{2,1,0:T(8,128)} %bitcast.18), calls=%async_computation.5 | async-start | bytes 2097152 | tf_op jit(solution)/shard_map/all_to_all | solution.py:915
  173.8 1.7 residual.1
  175.5 16.7 %all-to-all-done.5 = f32[128,16,128]{2,1,0:T(8,128)S(1)} async-done(((f32[128,16,128]{2,1,0:T(8,128)}), f32[128,16,128]{2,1,0:T(8,128)S(1)}, u32[]{:S(2)}, u32[]{:S(2)}) %all-to-all-start.5) | async-done | bytes 1048608 | tf_op jit(solution)/shard_map/all_to_all | solution.py:915
  (104 shorter events, 46.1 us)
Async XLA Ops:
  2.3 5.0 %collective-permute-start = (f32[8,8,128]{2,1,0:T(8,128)S(1)}, f32[8,8,128]{2,1,0:T(8,128)S(1)}, u32[]{:S(2)}, u32[]{:S(2)}) collective-permute-start(f32[8,8,128]{2,1,0:T(8,128)S(1)} %get-tuple-element.112), channel_id=1, source_target_pairs={{0,1},{1,0},{2,3},{3,2},{4,5},{5,4},{6,7},{7,6},{8,9},{9,8},{10,11... | collective-permute-start | bytes 98312 | tf_op jit(solution)/shard_map/ppermute | solution.py:898
  37.5 3.6 %collective-permute-start.5 = (f32[8,8,128]{2,1,0:T(8,128)S(1)}, f32[8,8,128]{2,1,0:T(8,128)S(1)}, u32[]{:S(2)}, u32[]{:S(2)}) collective-permute-start(f32[8,8,128]{2,1,0:T(8,128)S(1)} %get-tuple-element.122), channel_id=1, source_target_pairs={{0,1},{1,0},{2,3},{3,2},{4,5},{5,4},{6,7},{7,6},{8,9},{9,8},{10,11... | collective-permute-start | bytes 98312 | tf_op jit(solution)/shard_map/ppermute | solution.py:898
  38.0 3.4 %collective-permute-start.6 = (f32[8,8,128]{2,1,0:T(8,128)S(1)}, f32[8,8,128]{2,1,0:T(8,128)S(1)}, u32[]{:S(2)}, u32[]{:S(2)}) collective-permute-start(f32[8,8,128]{2,1,0:T(8,128)S(1)} %get-tuple-element.123), channel_id=1, source_target_pairs={{0,1},{1,0},{2,3},{3,2},{4,5},{5,4},{6,7},{7,6},{8,9},{9,8},{10,11... | collective-permute-start | bytes 98312 | tf_op jit(solution)/shard_map/ppermute | solution.py:898
  42.4 7.5 %collective-permute-start.10 = (f32[8,8,128]{2,1,0:T(8,128)S(1)}, f32[8,8,128]{2,1,0:T(8,128)S(1)}, u32[]{:S(2)}, u32[]{:S(2)}) collective-permute-start(f32[8,8,128]{2,1,0:T(8,128)S(1)} %get-tuple-element.129), channel_id=1, source_target_pairs={{0,16},{1,2},{2,1},{3,4},{4,3},{5,6},{6,5},{7,8},{8,7},{9,10},{10,... | collective-permute-start | bytes 98312 | tf_op jit(solution)/shard_map/ppermute | solution.py:898
  43.2 6.6 %collective-permute-start.11 = (f32[8,8,128]{2,1,0:T(8,128)S(1)}, f32[8,8,128]{2,1,0:T(8,128)S(1)}, u32[]{:S(2)}, u32[]{:S(2)}) collective-permute-start(f32[8,8,128]{2,1,0:T(8,128)S(1)} %get-tuple-element.130), channel_id=1, source_target_pairs={{0,1},{1,0},{2,3},{3,2},{4,5},{5,4},{6,7},{7,6},{8,9},{9,8},{10,11... | collective-permute-start | bytes 98312 | tf_op jit(solution)/shard_map/ppermute | solution.py:898
  44.3 5.6 %collective-permute-start.8 = (f32[8,8,128]{2,1,0:T(8,128)S(1)}, f32[8,8,128]{2,1,0:T(8,128)S(1)}, u32[]{:S(2)}, u32[]{:S(2)}) collective-permute-start(f32[8,8,128]{2,1,0:T(8,128)S(1)} %get-tuple-element.127), channel_id=1, source_target_pairs={{0,1},{1,0},{2,3},{3,2},{4,5},{5,4},{6,7},{7,6},{8,9},{9,8},{10,11... | collective-permute-start | bytes 98312 | tf_op jit(solution)/shard_map/ppermute | solution.py:898
  45.6 4.3 %collective-permute-start.9 = (f32[8,8,128]{2,1,0:T(8,128)S(1)}, f32[8,8,128]{2,1,0:T(8,128)S(1)}, u32[]{:S(2)}, u32[]{:S(2)}) collective-permute-start(f32[8,8,128]{2,1,0:T(8,128)S(1)} %get-tuple-element.128), channel_id=1, source_target_pairs={{0,16},{1,17},{2,18},{3,19},{4,20},{5,21},{6,22},{7,23},{8,24},{9,... | collective-permute-start | bytes 98312 | tf_op jit(solution)/shard_map/ppermute | solution.py:898
  69.5 3.5 %collective-permute-start.12 = (f32[8,8,128]{2,1,0:T(8,128)S(1)}, f32[8,8,128]{2,1,0:T(8,128)S(1)}, u32[]{:S(2)}, u32[]{:S(2)}) collective-permute-start(f32[8,8,128]{2,1,0:T(8,128)S(1)} %get-tuple-element.140), channel_id=1, source_target_pairs={{0,16},{1,2},{2,1},{3,4},{4,3},{5,6},{6,5},{7,8},{8,7},{9,10},{10,... | collective-permute-start | bytes 98312 | tf_op jit(solution)/shard_map/ppermute | solution.py:898
  70.3 3.6 %collective-permute-start.13 = (f32[8,8,128]{2,1,0:T(8,128)S(1)}, f32[8,8,128]{2,1,0:T(8,128)S(1)}, u32[]{:S(2)}, u32[]{:S(2)}) collective-permute-start(f32[8,8,128]{2,1,0:T(8,128)S(1)} %get-tuple-element.141), channel_id=1, source_target_pairs={{0,1},{1,0},{2,3},{3,2},{4,5},{5,4},{6,7},{7,6},{8,9},{9,8},{10,11... | collective-permute-start | bytes 98312 | tf_op jit(solution)/shard_map/ppermute | solution.py:898
  75.2 6.0 %collective-permute-start.16 = (f32[8,8,128]{2,1,0:T(8,128)S(1)}, f32[8,8,128]{2,1,0:T(8,128)S(1)}, u32[]{:S(2)}, u32[]{:S(2)}) collective-permute-start(f32[8,8,128]{2,1,0:T(8,128)S(1)} %get-tuple-element.150), channel_id=1, source_target_pairs={{0,16},{1,2},{2,1},{3,4},{4,3},{5,6},{6,5},{7,8},{8,7},{9,10},{10,... | collective-permute-start | bytes 98312 | tf_op jit(solution)/shard_map/ppermute | solution.py:898
  76.0 5.2 %collective-permute-start.17 = (f32[8,8,128]{2,1,0:T(8,128)S(1)}, f32[8,8,128]{2,1,0:T(8,128)S(1)}, u32[]{:S(2)}, u32[]{:S(2)}) collective-permute-start(f32[8,8,128]{2,1,0:T(8,128)S(1)} %get-tuple-element.151), channel_id=1, source_target_pairs={{0,1},{1,0},{2,3},{3,2},{4,5},{5,4},{6,7},{7,6},{8,9},{9,8},{10,11... | collective-permute-start | bytes 98312 | tf_op jit(solution)/shard_map/ppermute | solution.py:898
  77.1 4.1 %collective-permute-start.18 = (f32[8,8,128]{2,1,0:T(8,128)S(1)}, f32[8,8,128]{2,1,0:T(8,128)S(1)}, u32[]{:S(2)}, u32[]{:S(2)}) collective-permute-start(f32[8,8,128]{2,1,0:T(8,128)S(1)} %get-tuple-element.152), channel_id=1, source_target_pairs={{0,1},{1,0},{2,3},{3,2},{4,5},{5,4},{6,7},{7,6},{8,9},{9,8},{10,11... | collective-permute-start | bytes 98312 | tf_op jit(solution)/shard_map/ppermute | solution.py:898
  102.1 3.6 %collective-permute-start.20 = (f32[8,8,128]{2,1,0:T(8,128)S(1)}, f32[8,8,128]{2,1,0:T(8,128)S(1)}, u32[]{:S(2)}, u32[]{:S(2)}) collective-permute-start(f32[8,8,128]{2,1,0:T(8,128)S(1)} %get-tuple-element.162), channel_id=1, source_target_pairs={{0,16},{1,2},{2,1},{3,4},{4,3},{5,6},{6,5},{7,8},{8,7},{9,10},{10,... | collective-permute-start | bytes 98312 | tf_op jit(solution)/shard_map/ppermute | solution.py:898
  102.9 3.6 %collective-permute-start.21 = (f32[8,8,128]{2,1,0:T(8,128)S(1)}, f32[8,8,128]{2,1,0:T(8,128)S(1)}, u32[]{:S(2)}, u32[]{:S(2)}) collective-permute-start(f32[8,8,128]{2,1,0:T(8,128)S(1)} %get-tuple-element.163), channel_id=1, source_target_pairs={{0,1},{1,0},{2,3},{3,2},{4,5},{5,4},{6,7},{7,6},{8,9},{9,8},{10,11... | collective-permute-start | bytes 98312 | tf_op jit(solution)/shard_map/ppermute | solution.py:898
  103.4 3.4 %collective-permute-start.22 = (f32[8,8,128]{2,1,0:T(8,128)S(1)}, f32[8,8,128]{2,1,0:T(8,128)S(1)}, u32[]{:S(2)}, u32[]{:S(2)}) collective-permute-start(f32[8,8,128]{2,1,0:T(8,128)S(1)} %get-tuple-element.164), channel_id=1, source_target_pairs={{0,1},{1,0},{2,3},{3,2},{4,5},{5,4},{6,7},{7,6},{8,9},{9,8},{10,11... | collective-permute-start | bytes 98312 | tf_op jit(solution)/shard_map/ppermute | solution.py:898
  107.8 6.1 %collective-permute-start.24 = (f32[8,8,128]{2,1,0:T(8,128)S(1)}, f32[8,8,128]{2,1,0:T(8,128)S(1)}, u32[]{:S(2)}, u32[]{:S(2)}) collective-permute-start(f32[8,8,128]{2,1,0:T(8,128)S(1)} %get-tuple-element.175), channel_id=1, source_target_pairs={{0,16},{1,2},{2,1},{3,4},{4,3},{5,6},{6,5},{7,8},{8,7},{9,10},{10,... | collective-permute-start | bytes 98312 | tf_op jit(solution)/shard_map/ppermute | solution.py:898
  108.6 5.2 %collective-permute-start.25 = (f32[8,8,128]{2,1,0:T(8,128)S(1)}, f32[8,8,128]{2,1,0:T(8,128)S(1)}, u32[]{:S(2)}, u32[]{:S(2)}) collective-permute-start(f32[8,8,128]{2,1,0:T(8,128)S(1)} %get-tuple-element.176), channel_id=1, source_target_pairs={{0,1},{1,0},{2,3},{3,2},{4,5},{5,4},{6,7},{7,6},{8,9},{9,8},{10,11... | collective-permute-start | bytes 98312 | tf_op jit(solution)/shard_map/ppermute | solution.py:898
  109.7 4.2 %collective-permute-start.26 = (f32[8,8,128]{2,1,0:T(8,128)S(1)}, f32[8,8,128]{2,1,0:T(8,128)S(1)}, u32[]{:S(2)}, u32[]{:S(2)}) collective-permute-start(f32[8,8,128]{2,1,0:T(8,128)S(1)} %get-tuple-element.177), channel_id=1, source_target_pairs={{0,1},{1,0},{2,3},{3,2},{4,5},{5,4},{6,7},{7,6},{8,9},{9,8},{10,11... | collective-permute-start | bytes 98312 | tf_op jit(solution)/shard_map/ppermute | solution.py:898
  134.7 3.9 %collective-permute-start.28 = (f32[8,8,128]{2,1,0:T(8,128)S(1)}, f32[8,8,128]{2,1,0:T(8,128)S(1)}, u32[]{:S(2)}, u32[]{:S(2)}) collective-permute-start(f32[8,8,128]{2,1,0:T(8,128)S(1)} %get-tuple-element.187), channel_id=1, source_target_pairs={{0,16},{1,2},{2,1},{3,4},{4,3},{5,6},{6,5},{7,8},{8,7},{9,10},{10,... | collective-permute-start | bytes 98312 | tf_op jit(solution)/shard_map/ppermute | solution.py:898
  135.7 3.6 %collective-permute-start.29 = (f32[8,8,128]{2,1,0:T(8,128)S(1)}, f32[8,8,128]{2,1,0:T(8,128)S(1)}, u32[]{:S(2)}, u32[]{:S(2)}) collective-permute-start(f32[8,8,128]{2,1,0:T(8,128)S(1)} %get-tuple-element.188), channel_id=1, source_target_pairs={{0,1},{1,0},{2,3},{3,2},{4,5},{5,4},{6,7},{7,6},{8,9},{9,8},{10,11... | collective-permute-start | bytes 98312 | tf_op jit(solution)/shard_map/ppermute | solution.py:898
  140.6 6.0 %collective-permute-start.32 = (f32[8,8,128]{2,1,0:T(8,128)S(1)}, f32[8,8,128]{2,1,0:T(8,128)S(1)}, u32[]{:S(2)}, u32[]{:S(2)}) collective-permute-start(f32[8,8,128]{2,1,0:T(8,128)S(1)} %get-tuple-element.200), channel_id=1, source_target_pairs={{0,16},{1,2},{2,1},{3,4},{4,3},{5,6},{6,5},{7,8},{8,7},{9,10},{10,... | collective-permute-start | bytes 98312 | tf_op jit(solution)/shard_map/ppermute | solution.py:898
  141.5 5.2 %collective-permute-start.33 = (f32[8,8,128]{2,1,0:T(8,128)S(1)}, f32[8,8,128]{2,1,0:T(8,128)S(1)}, u32[]{:S(2)}, u32[]{:S(2)}) collective-permute-start(f32[8,8,128]{2,1,0:T(8,128)S(1)} %get-tuple-element.201), channel_id=1, source_target_pairs={{0,1},{1,0},{2,3},{3,2},{4,5},{5,4},{6,7},{7,6},{8,9},{9,8},{10,11... | collective-permute-start | bytes 98312 | tf_op jit(solution)/shard_map/ppermute | solution.py:898
  142.5 4.1 %collective-permute-start.34 = (f32[8,8,128]{2,1,0:T(8,128)S(1)}, f32[8,8,128]{2,1,0:T(8,128)S(1)}, u32[]{:S(2)}, u32[]{:S(2)}) collective-permute-start(f32[8,8,128]{2,1,0:T(8,128)S(1)} %get-tuple-element.202), channel_id=1, source_target_pairs={{0,1},{1,0},{2,3},{3,2},{4,5},{5,4},{6,7},{7,6},{8,9},{9,8},{10,11... | collective-permute-start | bytes 98312 | tf_op jit(solution)/shard_map/ppermute | solution.py:898
  169.2 23.1 %all-to-all-start.5 = ((f32[128,16,128]{2,1,0:T(8,128)}), f32[128,16,128]{2,1,0:T(8,128)S(1)}, u32[]{:S(2)}, u32[]{:S(2)}) async-start(f32[128,16,128]{2,1,0:T(8,128)} %bitcast.18), calls=%async_computation.5 | async-start | bytes 2097152 | tf_op jit(solution)/shard_map/all_to_all | solution.py:915
  (18 other events, 226.7 us)
